TPU v7x, 256 devices: a whole 4x4x8 slice. The times are simulated.
256 devices in a mesh: grp: 4 (over x_hi, core), tile: 64 (over z, x_lo, y).
Axes of the slice: x: 4 (x_hi: 2, x_lo: 2; x = x_hi * 2 + x_lo), y: 4, z: 8, core: 2. Of those that a mesh axis runs over, the one named last changes fastest.
Arguments:
- sky: float32 [32, 8192], P(None, 'tile'), may hold values from -6 to 6
- psf_basis: bfloat16 [4, 5, 41, 41], P('grp'), may hold values from -0.15625 to 0.15625
- item_tile: int32 [768], P(('grp', 'tile')), may hold values from 0 to 63, as said below
- warp_corner: int32 [768, 32, 128], P(('grp', 'tile')), may hold values from 0 to 5454, as said below
- warp_weight: bfloat16 [768, 4, 32, 128], P(('grp', 'tile')), may hold values from 0 to 0.5
- psf_coeff: bfloat16 [768, 32, 5, 128], P(('grp', 'tile')), may hold values from -3 to 3
- observed: bfloat16 [768, 32, 128], P(('grp', 'tile')), may hold values from -6 to 6
- inv_var: bfloat16 [768, 32, 128], P(('grp', 'tile')), may hold values from 0.25 to 2
Outputs:
- new_sky: float32 [32, 8192], P(None, 'tile')
Inputs may be any that keep to these rules, and one draw needn't show every extreme that they name: `item_tile`: the footprints of the device at index d of tile are its block of 3 consecutive entries; each names a tile of d - 1 to d + 1, the first of every block d itself. `warp_corner`: each value at pixel (r, c) is q * 176 + p with q at most 30, q within 3 of r, and p at most 174.
All inputs are finite; a program needn't handle non-finite values.
Results may differ from a plain program's by a relative error of at most 0.0003.
Values sent between devices are 32-bit elements; how exact they have to be, the bound alone decides.
A program may use at most 128 MiB of HBM per device.

v0:
```python
import jax
import jax.numpy as jnp
from jax import lax
from jax.sharding import PartitionSpec as P

MARGIN = 24


step_size = 0.25
band_rows = 8


def shifted(value, axis, steps):
    count = lax.axis_size(axis)
    first, last = (max(0, -steps), min(count, count - steps))
    return lax.ppermute(value, axis, [(source, source + steps) for source in range(first, last)])


def fetch_near(sky, margin):
    tile_cols = sky.shape[1]
    received = []
    for offset, lower, upper in (
        (2, tile_cols - margin, tile_cols),
        (1, 0, tile_cols),
        (-1, 0, tile_cols),
        (-2, 0, margin),
    ):
        received.append(shifted(sky[:, lower:upper], "tile", offset))
    return [received[0], received[1], sky, received[2], received[3]]


def return_near(gradient, tile_cols, margin):
    owned = gradient[:, margin + tile_cols : margin + 2 * tile_cols]
    pieces = (
        (-2, 0, margin, tile_cols - margin),
        (-1, margin, margin + tile_cols, 0),
        (1, margin + 2 * tile_cols, margin + 3 * tile_cols, 0),
        (2, margin + 3 * tile_cols, 2 * margin + 3 * tile_cols, 0),
    )
    for offset, lower, upper, place in pieces:
        arrived = shifted(gradient[:, lower:upper], "tile", offset)
        owned = owned + jnp.pad(arrived, ((0, 0), (place, tile_cols - place - (upper - lower))))
    return owned


def psf_matrices(eigen_psf, tile_cols):
    psf_count, tap_count = (eigen_psf.shape[0], eigen_psf.shape[1])
    middle = tap_count // 2
    grid_shape = (tap_count, tile_cols, tile_cols)
    tap_level = lax.broadcasted_iota(jnp.int32, grid_shape, 0)
    target = lax.broadcasted_iota(jnp.int32, grid_shape, 1)
    source = lax.broadcasted_iota(jnp.int32, grid_shape, 2)
    selector = (target - source + middle == tap_level).astype(jnp.float32)
    tap_table = jnp.einsum(
        "kab,bji->kaji", eigen_psf.astype(jnp.float32), selector, precision=lax.Precision.HIGHEST
    )
    forward_matrix = tap_table.transpose(1, 2, 0, 3).reshape(
        tap_count * tile_cols, psf_count * tile_cols
    )
    adjoint_matrix = tap_table.transpose(1, 0, 3, 2).reshape(
        tap_count * psf_count * tile_cols, tile_cols
    )
    return (forward_matrix, adjoint_matrix)


def stencil_table(corner, weight, extent):
    pixel_rows, tile_cols = corner.shape
    corner_row = corner // extent
    corner_col = corner % extent
    row_iota = lax.broadcasted_iota(jnp.int32, corner.shape, 0)
    base = (corner_row - row_iota + 3) * extent + corner_col
    slots = lax.broadcasted_iota(jnp.int32, (pixel_rows, tile_cols, band_rows * extent), 2)
    weight_f = weight.astype(jnp.float32)
    table = jnp.zeros((pixel_rows, tile_cols, band_rows * extent), jnp.float32)
    for number, jump in enumerate((0, 1, extent, extent + 1)):
        hit = slots == (base + jump)[:, :, None]
        table = table + jnp.where(hit, weight_f[number][:, :, None], 0.0)
    return table


def per_device(sky, psf_basis, item_tile, warp_corner, warp_weight, psf_coeff, observed, inv_var):
    pixel_rows, tile_cols = sky.shape
    margin = MARGIN
    extent = tile_cols + 2 * margin
    own_index = lax.axis_index("tile")
    region = jnp.concatenate(fetch_near(sky, margin), axis=1)
    region_width = region.shape[1]
    item_count = warp_corner.shape[0]
    start_cols = (item_tile - (own_index - 1)) * tile_cols

    def warp_one(number, collected):
        window = lax.dynamic_slice_in_dim(region, start_cols[number], extent, 1)
        padded = jnp.pad(window, ((3, band_rows - 4), (0, 0)))
        band = jnp.stack(
            [padded[offset : offset + pixel_rows] for offset in range(band_rows)], axis=1
        ).reshape(pixel_rows, band_rows * extent)
        table = stencil_table(warp_corner[number], warp_weight[number], extent)
        values = jnp.einsum("ri,rci->rc", band, table, precision=lax.Precision.HIGHEST)
        return collected.at[number].set(values)

    warped = lax.fori_loop(
        0, item_count, warp_one, jnp.zeros((item_count, pixel_rows, tile_cols), jnp.float32)
    )
    eigen_psf = psf_basis[0]
    psf_count, tap_count = (eigen_psf.shape[0], eigen_psf.shape[1])
    middle = tap_count // 2
    forward_matrix, adjoint_matrix = psf_matrices(eigen_psf, tile_cols)
    lifted = jnp.pad(warped, ((0, 0), (middle, middle), (0, 0)))
    stacked = jnp.stack(
        [lifted[:, offset : offset + pixel_rows] for offset in range(tap_count)], axis=2
    )
    stacked = stacked.reshape(item_count * pixel_rows, tap_count * tile_cols)
    blurred = jnp.dot(stacked, forward_matrix, precision=lax.Precision.HIGHEST)
    blurred = blurred.reshape(item_count, pixel_rows, psf_count, tile_cols)
    coeff_f = psf_coeff.astype(jnp.float32)
    predicted = jnp.sum(blurred * coeff_f, axis=2)
    misfit = inv_var.astype(jnp.float32) * (predicted - observed.astype(jnp.float32))
    weighted = coeff_f * misfit[:, :, None, :]
    lowered = jnp.pad(weighted, ((0, 0), (middle, middle), (0, 0), (0, 0)))
    stacked_back = jnp.stack(
        [
            lowered[:, 2 * middle - offset : 2 * middle - offset + pixel_rows]
            for offset in range(tap_count)
        ],
        axis=2,
    )
    stacked_back = stacked_back.reshape(item_count * pixel_rows, tap_count * psf_count * tile_cols)
    backward = jnp.dot(stacked_back, adjoint_matrix, precision=lax.Precision.HIGHEST)
    backward = backward.reshape(item_count, pixel_rows, tile_cols)

    def spread_one(number, gathered):
        table = stencil_table(warp_corner[number], warp_weight[number], extent)
        band_grad = jnp.einsum(
            "rc,rci->ri", backward[number], table, precision=lax.Precision.HIGHEST
        ).reshape(pixel_rows, band_rows, extent)
        padded = jnp.zeros((pixel_rows + band_rows - 1, extent), jnp.float32)
        for offset in range(band_rows):
            padded = padded.at[offset : offset + pixel_rows].add(band_grad[:, offset])
        window_grad = padded[3 : 3 + pixel_rows]
        current = lax.dynamic_slice_in_dim(gathered, start_cols[number], extent, 1)
        return lax.dynamic_update_slice_in_dim(
            gathered, current + window_grad, start_cols[number], 1
        )

    gradient = lax.fori_loop(
        0, item_count, spread_one, jnp.zeros((pixel_rows, region_width), jnp.float32)
    )
    owned = return_near(gradient, tile_cols, margin)
    total = lax.psum(owned, "grp")
    return sky - step_size * total


def solution(mesh):
    return jax.shard_map(
        per_device,
        mesh=mesh,
        in_specs=(
            P(None, "tile"),
            P("grp", None, None, None),
            P(("grp", "tile")),
            P(("grp", "tile"), None, None),
            P(("grp", "tile"), None, None, None),
            P(("grp", "tile"), None, None, None),
            P(("grp", "tile"), None, None),
            P(("grp", "tile"), None, None),
        ),
        out_specs=P(None, "tile"),
        check_vma=False,
    )
```

profile of v0, /device:TPU:129, one launch (start us, length us, event | category | flops | bytes accessed | tf_op | source)
XLA Modules:
  0.0 350.6 jit_solution(11282713989028379084)
XLA Ops:
  0.0 3.3 collective-permute-start.1
  3.3 6.3 %collective-permute-start.2 = (f32[32,128]{1,0:T(8,128)}, f32[32,128]{1,0:T(8,128)S(1)}, u32[]{:S(2)}, u32[]{:S(2)}) collective-permute-start(f32[32,128]{1,0:T(8,128)} %param.30), channel_id=1, source_target_pairs={{1,0},{2,1},{3,2},{4,3},{5,4},{6,5},{7,6},{8,7},{9,8},{10,9},{11,1... | collective-permute-start | bytes 49160 | tf_op jit(solution)/shard_map/ppermute | solution.py:16
  12.4 7.9 %collective-permute-start.3 = (f32[32,24]{1,0:T(8,128)S(1)}, f32[32,24]{1,0:T(8,128)S(1)}, u32[]{:S(2)}, u32[]{:S(2)}) collective-permute-start(f32[32,24]{1,0:T(8,128)S(1)} %get-tuple-element.629), channel_id=1, source_target_pairs={{2,0},{3,1},{4,2},{5,3},{6,4},{7,5},{8,6},{9,7},{10,8},{11,9},{12,... | collective-permute-start | bytes 9224 | tf_op jit(solution)/shard_map/ppermute | solution.py:16
  20.3 7.7 %fusion.69 = f32[128,128,5,41]{1,3,2,0:T(8,128)} fusion(bf16[1,5,41,41]{3,2,1,0:T(8,128)(2,1)S(1)} %copy-done), kind=kOutput, calls=%fused_computation.172 | convolution fusion | flops 277430272 | bytes 13451690 | tf_op jit(solution)/shard_map/kab,bji->kaji/dot_general | solution.py:54
  28.0 15.8 %copy.21 = f32[41,128,5,128]{1,0,3,2:T(8,128)} copy(f32[41,128,5,128]{3,0,2,1:T(8,128)} %bitcast.554) | data formatting | bytes 26869760 | tf_op jit(solution)/shard_map/transpose | solution.py:57
  43.8 16.7 %copy.72 = f32[80,8,41,128]{3,1,2,0:T(8,128)} copy(f32[80,8,41,128]{3,2,1,0:T(8,128)} %bitcast.556) | data formatting | bytes 26869760
  60.7 125.9 %while.40 = (s32[]{:T(128)}, f32[3,32,128]{2,1,0:T(8,128)S(1)}, s32[3]{0:T(128)S(1)}, f32[32,432]{1,0:T(8,128)S(1)}, s32[3,32,128]{2,1,0:T(8,128)S(1)}, /*index=...) while((s32[]{:T(128)}, f32[3,32,128]{2,1,0:T(8,128)S(1)}, ...), condition=%wide.region_2.3_spmd, body=%wide.region_0.2_spmd.sunk | while | flops 132743184 | bytes 48122052 | solution.py:101
  61.0 13.8 %fusion.246 = f32[32,128,1408]{2,1,0:T(8,128)} fusion(f32[32,128]{1,0:T(8,128)S(1)} %get-tuple-element.723, s32[32,128]{1,0:T(8,128)S(1)} %get-tuple-element.725, f32[32,128]{1,0:T(8,128)S(1)} %get-tuple-element.726, s32[32,128]{1,0:T(8,128)S(1)} %get-tuple-element.727, f32[32,128]{1,0:T(8,128)S(1)} %get-tuple-element.728, ...), kind=kLoop, calls=%fused_computation.1.clone.1.clone.1 | loop fusion | flops 63438848 | bytes 23199744 | tf_op jit(solution)/shard_map/while/body/eval_jaxpr/ri,rci->rc/dot_general | solution.py:98
  78.2 23.2 %fusion.247 = f32[32,1,128]{2,1,0:T(1,128)S(1)} fusion(f32[32,1408,1]{1,2,0:T(1,128)S(1)} %reshape.819, f32[32,128,1408]{2,1,0:T(8,128)} %fusion.246), kind=kOutput, calls=%fused_computation.clone.2 | convolution fusion | flops 69206016 | bytes 23265280 | tf_op jit(solution)/shard_map/while/body/eval_jaxpr/ri,rci->rc/dot_general | solution.py:98
  102.9 13.8 %fusion.246 = f32[32,128,1408]{2,1,0:T(8,128)} fusion(f32[32,128]{1,0:T(8,128)S(1)} %get-tuple-element.723, s32[32,128]{1,0:T(8,128)S(1)} %get-tuple-element.725, f32[32,128]{1,0:T(8,128)S(1)} %get-tuple-element.726, s32[32,128]{1,0:T(8,128)S(1)} %get-tuple-element.727, f32[32,128]{1,0:T(8,128)S(1)} %get-tuple-element.728, ...), kind=kLoop, calls=%fused_computation.1.clone.1.clone.1 | loop fusion | flops 63438848 | bytes 23199744 | tf_op jit(solution)/shard_map/while/body/eval_jaxpr/ri,rci->rc/dot_general | solution.py:98
  120.1 23.2 %fusion.247 = f32[32,1,128]{2,1,0:T(1,128)S(1)} fusion(f32[32,1408,1]{1,2,0:T(1,128)S(1)} %reshape.819, f32[32,128,1408]{2,1,0:T(8,128)} %fusion.246), kind=kOutput, calls=%fused_computation.clone.2 | convolution fusion | flops 69206016 | bytes 23265280 | tf_op jit(solution)/shard_map/while/body/eval_jaxpr/ri,rci->rc/dot_general | solution.py:98
  144.8 13.8 %fusion.246 = f32[32,128,1408]{2,1,0:T(8,128)} fusion(f32[32,128]{1,0:T(8,128)S(1)} %get-tuple-element.723, s32[32,128]{1,0:T(8,128)S(1)} %get-tuple-element.725, f32[32,128]{1,0:T(8,128)S(1)} %get-tuple-element.726, s32[32,128]{1,0:T(8,128)S(1)} %get-tuple-element.727, f32[32,128]{1,0:T(8,128)S(1)} %get-tuple-element.728, ...), kind=kLoop, calls=%fused_computation.1.clone.1.clone.1 | loop fusion | flops 63438848 | bytes 23199744 | tf_op jit(solution)/shard_map/while/body/eval_jaxpr/ri,rci->rc/dot_general | solution.py:98
  162.0 23.2 %fusion.247 = f32[32,1,128]{2,1,0:T(1,128)S(1)} fusion(f32[32,1408,1]{1,2,0:T(1,128)S(1)} %reshape.819, f32[32,128,1408]{2,1,0:T(8,128)} %fusion.246), kind=kOutput, calls=%fused_computation.clone.2 | convolution fusion | flops 69206016 | bytes 23265280 | tf_op jit(solution)/shard_map/while/body/eval_jaxpr/ri,rci->rc/dot_general | solution.py:98
  190.0 15.8 %fusion.77 = f32[3,32,128]{2,1,0:T(8,128)S(1)} fusion(f32[5,128,5248,1]{2,1,0,3:T(8,128)} %bitcast.557, f32[3,32,5248,1]{2,1,0,3:T(8,128)} %reshape.810, bf16[3,32,5,128]{3,1,2,0:T(8,128)(2,1)S(1)} %copy-done.2), kind=kOutput, calls=%fused_computation.177 | convolution fusion | flops 3869417472 | bytes 15622144 | tf_op jit(solution)/shard_map/dot_general | solution.py:113
  207.0 19.2 %fusion.80 = f32[3,32,128]{2,1,0:T(8,128)S(1)} fusion(f32[3,32,41,5,128]{4,1,3,0,2:T(8,128)S(1)} %fusion.162, f32[41,5,128,128,1]{2,0,1,3,4:T(8,128)} %bitcast.555), kind=kOutput, calls=%fused_computation.178 | convolution fusion | flops 3869245440 | bytes 23560192 | tf_op jit(solution)/shard_map/dot_general | solution.py:128
  226.2 91.9 %while.41 = (s32[]{:T(128)}, f32[32,432]{1,0:T(8,128)S(1)}, s32[3]{0:T(128)S(1)}, f32[3,32,128]{2,1,0:T(8,128)S(1)}, s32[3,32,128]{2,1,0:T(8,128)S(1)}, /*index=...) while((s32[]{:T(128)}, f32[32,432]{1,0:T(8,128)S(1)}, ...), condition=%wide.region_5.6_spmd, body=%wide.region_4.5_spmd.sunk | while | flops 132784128 | bytes 2765879 | solution.py:145
  226.3 25.0 %fusion.251 = f32[32,1,1408]{2,1,0:T(1,128)S(1)} fusion(f32[32,128,1]{1,2,0:T(1,128)S(1)} %bitcast.562, f32[32,128]{1,0:T(8,128)S(1)} %get-tuple-element.737, s32[32,128]{1,0:T(8,128)S(1)} %get-tuple-element.739, f32[32,128]{1,0:T(8,128)S(1)} %get-tuple-element.740, s32[32,128]{1,0:T(8,128)S(1)} %get-tuple-element.741, ...), kind=kOutput, calls=%fused_computation.68.clone.1 | convolution fusion | flops 132644864 | bytes 327680 | tf_op jit(solution)/shard_map/while/body/eval_jaxpr/rc,rci->ri/dot_general | solution.py:133
  256.9 25.0 %fusion.251 = f32[32,1,1408]{2,1,0:T(1,128)S(1)} fusion(f32[32,128,1]{1,2,0:T(1,128)S(1)} %bitcast.562, f32[32,128]{1,0:T(8,128)S(1)} %get-tuple-element.737, s32[32,128]{1,0:T(8,128)S(1)} %get-tuple-element.739, f32[32,128]{1,0:T(8,128)S(1)} %get-tuple-element.740, s32[32,128]{1,0:T(8,128)S(1)} %get-tuple-element.741, ...), kind=kOutput, calls=%fused_computation.68.clone.1 | convolution fusion | flops 132644864 | bytes 327680 | tf_op jit(solution)/shard_map/while/body/eval_jaxpr/rc,rci->ri/dot_general | solution.py:133
  287.5 25.0 %fusion.251 = f32[32,1,1408]{2,1,0:T(1,128)S(1)} fusion(f32[32,128,1]{1,2,0:T(1,128)S(1)} %bitcast.562, f32[32,128]{1,0:T(8,128)S(1)} %get-tuple-element.737, s32[32,128]{1,0:T(8,128)S(1)} %get-tuple-element.739, f32[32,128]{1,0:T(8,128)S(1)} %get-tuple-element.740, s32[32,128]{1,0:T(8,128)S(1)} %get-tuple-element.741, ...), kind=kOutput, calls=%fused_computation.68.clone.1 | convolution fusion | flops 132644864 | bytes 327680 | tf_op jit(solution)/shard_map/while/body/eval_jaxpr/rc,rci->ri/dot_general | solution.py:133
  318.2 1.9 collective-permute-start.5
  320.1 3.4 collective-permute-start.6
  325.5 4.9 %collective-permute-start.7 = (f32[32,24]{1,0:T(8,128)S(1)}, f32[32,24]{1,0:T(8,128)S(1)}, u32[]{:S(2)}, u32[]{:S(2)}) collective-permute-start(f32[32,24]{1,0:T(8,128)S(1)} %get-tuple-element.626), channel_id=1, source_target_pairs={{0,2},{1,3},{2,4},{3,5},{4,6},{5,7},{6,8},{7,9},{8,10},{9,11},{10,... | collective-permute-start | bytes 9224 | tf_op jit(solution)/shard_map/ppermute | solution.py:16
  330.3 4.1 %collective-permute-done.7 = f32[32,24]{1,0:T(8,128)S(1)} collective-permute-done((f32[32,24]{1,0:T(8,128)S(1)}, f32[32,24]{1,0:T(8,128)S(1)}, u32[]{:S(2)}, u32[]{:S(2)}) %collective-permute-start.7) | collective-permute-done | bytes 3104 | tf_op jit(solution)/shard_map/ppermute | solution.py:16
  334.5 15.5 %psum.7 = f32[32,128]{1,0:T(8,128)S(1)} all-reduce(f32[32,128]{1,0:T(8,128)S(1)} %pad_add_fusion), channel_id=1, replica_groups=mesh['grp'=4,'tile'=64] {'grp'}, use_global_device_ids=true, to_apply=%region_6.7 | all-reduce | flops 4096 | bytes 32768 | tf_op jit(solution)/shard_map/psum | solution.py:149
  (261 shorter events, 28.5 us)
Async XLA Ops:
  0.0 20.3 %copy-start = (bf16[1,5,41,41]{3,2,1,0:T(8,128)(2,1)S(1)}, bf16[1,5,41,41]{3,2,1,0:T(8,128)(2,1)}, u32[]{:S(2)}) copy-start(bf16[1,5,41,41]{3,2,1,0:T(8,128)(2,1)} %param.31) | copy-start | bytes 50434
  0.0 28.0 %copy-start.10 = (s32[3]{0:T(128)S(1)}, s32[3]{0:T(128)}, u32[]{:S(2)}) copy-start(s32[3]{0:T(128)} %param.32) | copy-start | bytes 40
  0.0 60.5 %collective-permute-start.1 = (f32[32,128]{1,0:T(8,128)}, f32[32,128]{1,0:T(8,128)S(1)}, u32[]{:S(2)}, u32[]{:S(2)}) collective-permute-start(f32[32,128]{1,0:T(8,128)} %param.30), channel_id=1, source_target_pairs={{0,1},{1,2},{2,3},{3,4},{4,5},{5,6},{6,7},{7,8},{8,9},{9,10},{10,1... | collective-permute-start | bytes 49160 | tf_op jit(solution)/shard_map/ppermute | solution.py:16
  3.3 57.2 %collective-permute-start.2 = (f32[32,128]{1,0:T(8,128)}, f32[32,128]{1,0:T(8,128)S(1)}, u32[]{:S(2)}, u32[]{:S(2)}) collective-permute-start(f32[32,128]{1,0:T(8,128)} %param.30), channel_id=1, source_target_pairs={{1,0},{2,1},{3,2},{4,3},{5,4},{6,5},{7,6},{8,7},{9,8},{10,9},{11,1... | collective-permute-start | bytes 49160 | tf_op jit(solution)/shard_map/ppermute | solution.py:16
  10.5 50.1 %collective-permute-start = (f32[32,24]{1,0:T(8,128)S(1)}, f32[32,24]{1,0:T(8,128)S(1)}, u32[]{:S(2)}, u32[]{:S(2)}) collective-permute-start(f32[32,24]{1,0:T(8,128)S(1)} %get-tuple-element.630), channel_id=1, source_target_pairs={{0,2},{1,3},{2,4},{3,5},{4,6},{5,7},{6,8},{7,9},{8,10},{9,11},{10,... | collective-permute-start | bytes 9224 | tf_op jit(solution)/shard_map/ppermute | solution.py:16
  12.4 48.1 %collective-permute-start.3 = (f32[32,24]{1,0:T(8,128)S(1)}, f32[32,24]{1,0:T(8,128)S(1)}, u32[]{:S(2)}, u32[]{:S(2)}) collective-permute-start(f32[32,24]{1,0:T(8,128)S(1)} %get-tuple-element.629), channel_id=1, source_target_pairs={{2,0},{3,1},{4,2},{5,3},{6,4},{7,5},{8,6},{9,7},{10,8},{11,9},{12,... | collective-permute-start | bytes 9224 | tf_op jit(solution)/shard_map/ppermute | solution.py:16
  43.8 16.7 %copy-start.5 = (f32[32,128]{1,0:T(8,128)S(1)}, f32[32,128]{1,0:T(8,128)}, u32[]{:S(2)}) copy-start(f32[32,128]{1,0:T(8,128)} %param.30) | copy-start | bytes 49156
  43.8 16.8 %copy-start.3 = (bf16[3,4,32,128]{3,2,1,0:T(8,128)(2,1)S(1)}, bf16[3,4,32,128]{3,2,1,0:T(8,128)(2,1)}, u32[]{:S(2)}) copy-start(bf16[3,4,32,128]{3,2,1,0:T(8,128)(2,1)} %param.34) | copy-start | bytes 294916
  43.8 16.9 %copy-start.4 = (s32[3,32,128]{2,1,0:T(8,128)S(1)}, s32[3,32,128]{2,1,0:T(8,128)}, u32[]{:S(2)}) copy-start(s32[3,32,128]{2,1,0:T(8,128)} %param.33) | copy-start | bytes 147460
  43.8 16.9 %copy-start.9 = (s32[3]{0:T(128)S(1)}, s32[3]{0:T(128)}, u32[]{:S(2)}) copy-start(s32[3]{0:T(128)} %constant.653.clone.1) | copy-start | bytes 40
  186.6 3.3 copy-start.2
  188.5 17.3 %copy-start.7 = (bf16[3,32,128]{2,1,0:T(8,128)(2,1)S(1)}, bf16[3,32,128]{2,1,0:T(8,128)(2,1)}, u32[]{:S(2)}) copy-start(bf16[3,32,128]{2,1,0:T(8,128)(2,1)} %param.36) | copy-start | bytes 73732
  188.5 17.3 %copy-start.8 = (bf16[3,32,128]{2,1,0:T(8,128)(2,1)S(1)}, bf16[3,32,128]{2,1,0:T(8,128)(2,1)}, u32[]{:S(2)}) copy-start(bf16[3,32,128]{2,1,0:T(8,128)(2,1)} %param.37) | copy-start | bytes 73732
  226.2 123.8 %copy-start.6 = (f32[32,128]{1,0:T(8,128)S(1)}, f32[32,128]{1,0:T(8,128)}, u32[]{:S(2)}) copy-start(f32[32,128]{1,0:T(8,128)} %param.30) | copy-start | bytes 49156
  318.1 32.5 %copy-start.1 = (bf16[1,5,41,41]{3,2,1,0:T(8,128)(2,1)S(1)}, bf16[1,5,41,41]{3,2,1,0:T(8,128)(2,1)}, u32[]{:S(2)}) copy-start(bf16[1,5,41,41]{3,2,1,0:T(8,128)(2,1)} %param.31) | copy-start | bytes 50434
  318.2 16.3 %collective-permute-start.5 = (f32[32,128]{1,0:T(8,128)S(1)}, f32[32,128]{1,0:T(8,128)S(1)}, u32[]{:S(2)}, u32[]{:S(2)}) collective-permute-start(f32[32,128]{1,0:T(8,128)S(1)} %get-tuple-element.627), channel_id=1, source_target_pairs={{1,0},{2,1},{3,2},{4,3},{5,4},{6,5},{7,6},{8,7},{9,8},{10,9},{11,1... | collective-permute-start | bytes 49160 | tf_op jit(solution)/shard_map/ppermute | solution.py:16
  320.1 14.4 %collective-permute-start.6 = (f32[32,128]{1,0:T(8,128)S(1)}, f32[32,128]{1,0:T(8,128)S(1)}, u32[]{:S(2)}, u32[]{:S(2)}) collective-permute-start(f32[32,128]{1,0:T(8,128)S(1)} %get-tuple-element.628), channel_id=1, source_target_pairs={{0,1},{1,2},{2,3},{3,4},{4,5},{5,6},{6,7},{7,8},{8,9},{9,10},{10,1... | collective-permute-start | bytes 49160 | tf_op jit(solution)/shard_map/ppermute | solution.py:16
  323.5 6.8 %collective-permute-start.4 = (f32[32,24]{1,0:T(8,128)S(1)}, f32[32,24]{1,0:T(8,128)S(1)}, u32[]{:S(2)}, u32[]{:S(2)}) collective-permute-start(f32[32,24]{1,0:T(8,128)S(1)} %get-tuple-element.625), channel_id=1, source_target_pairs={{2,0},{3,1},{4,2},{5,3},{6,4},{7,5},{8,6},{9,7},{10,8},{11,9},{12,... | collective-permute-start | bytes 9224 | tf_op jit(solution)/shard_map/ppermute | solution.py:16
  325.5 9.0 %collective-permute-start.7 = (f32[32,24]{1,0:T(8,128)S(1)}, f32[32,24]{1,0:T(8,128)S(1)}, u32[]{:S(2)}, u32[]{:S(2)}) collective-permute-start(f32[32,24]{1,0:T(8,128)S(1)} %get-tuple-element.626), channel_id=1, source_target_pairs={{0,2},{1,3},{2,4},{3,5},{4,6},{5,7},{6,8},{7,9},{8,10},{9,11},{10,... | collective-permute-start | bytes 9224 | tf_op jit(solution)/shard_map/ppermute | solution.py:16
where the time goes:
time: 355 us; the launch traced here: 351 us
  matrix products  187 us (53%)
  local copies, waits for them, and re-layouts  51.5 us (15%)
  other arithmetic  47.2 us (13%)
  starting transfers between devices  31.5 us (9%)
  blocking collectives  15.5 us (4%)
  loops' own time  12.5 us (4%)
  waiting for transfers between devices  4.13 us (1%)
    dot_general x3, matrix products, spread_one(): jnp.einsum('rc,rci->ri', backward[number], table, precision=lax.Precision...  75 us
    dot_general x3, matrix products, warp_one(): jnp.einsum('ri,rci->rc', band, table, precision=lax.Precision.HIGHEST)  69.7 us
    dot_general x3, other arithmetic, warp_one(): jnp.einsum('ri,rci->rc', band, table, precision=lax.Precision.HIGHEST)  41.5 us
    ppermute x8, starting transfers between devices, shifted(): lax.ppermute(value, axis, [(source, source + steps) for source in range(f...  31.5 us
    dot_general x1, matrix products, per_device(): jnp.dot(stacked_back, adjoint_matrix, precision=lax.Precision.HIGHEST)  19.2 us
    unnamed x102, local copies, waits for them, and re-layouts  17.8 us
    transpose x1, local copies, waits for them, and re-layouts, psf_matrices(): tap_table.transpose(1, 2, 0, 3)  15.8 us
    dot_general x1, matrix products, per_device(): blurred = jnp.dot(stacked, forward_matrix, precision=lax.Precision.HIGHEST)  15.8 us
  transfers between devices with their start and end apart: 8, of which 1 were waited for; matrix products, arithmetic and copies ran while one was open for 12% of the time, Pallas kernels for 0%

commit v1 on v0

v1 whole, which is shorter than its diff:
```python
import functools

import jax
import jax.numpy as jnp
from jax import lax
from jax.experimental import pallas as pl
from jax.experimental.pallas import tpu as pltpu
from jax.sharding import PartitionSpec as P

F32, BF16, I32 = jnp.float32, jnp.bfloat16, jnp.int32
ROWS, COLS, MARGIN, TAPS, NPSF, ITEMS = 32, 128, 24, 41, 5, 3
EXTENT = COLS + 2 * MARGIN
HALF = TAPS // 2
WIDE = ITEMS * COLS
DEPTH = TAPS * ROWS
GROUPS_OF_4 = (TAPS + 3) // 4
PAD = 8
STEP = 0.25
OFFSETS = (-2, -1, 1, 2)
SLOT = {-2: 0, -1: 1, 0: 2, 1: 3, 2: 4}


def split(value):
    high = value.astype(BF16)
    return high, (value - high.astype(F32)).astype(BF16)


def nt_dot(a, b):
    return lax.dot_general(a, b, (((1,), (1,)), ((), ())), preferred_element_type=F32)


def prepare(psf, corner, coeff, tap_rows, tap_cols, blur_left, blur_right, coeff_wide, coeff_f, hot):
    tap_rows[...] = jnp.zeros_like(tap_rows)
    for k in range(NPSF):
        tap_rows[k, pl.ds(0, TAPS), pl.ds(0, TAPS)] = psf[0, k].astype(F32)
    for k in range(NPSF):
        tap_cols[k] = pltpu.roll(tap_rows[k], 4, 0).T
    lane_group = lax.broadcasted_iota(I32, (8, COLS), 1) // ROWS

    def tap_tile(j, _):
        whole = []
        for k in range(NPSF):
            for r0 in range(0, ROWS, 8):
                tile = jnp.zeros((8, COLS), F32)
                for part in range(4):
                    row = jnp.broadcast_to(tap_cols[k, pl.ds(4 * j + part, 1), :], (8, COLS))
                    turned = pltpu.roll(row, (r0 + ROWS * part - HALF - 4) % COLS, 1, stride=1, stride_axis=0)
                    tile = turned if part == 0 else jnp.where(lane_group == part, turned, tile)
                whole.append(tile)
        whole = jnp.concatenate(whole, axis=0)
        at = pl.multiple_of(j * COLS, COLS)
        blur_left[:, pl.ds(at, COLS)] = whole.astype(BF16)
        blur_right[pl.ds(at, COLS), :] = whole.T.astype(BF16)
        return 0

    lax.fori_loop(0, GROUPS_OF_4, tap_tile, 0)
    for n in range(ITEMS):
        coeff_wide[:, pl.ds(0, NPSF), :] = coeff[n].astype(F32)
        for k in range(NPSF):
            coeff_f[k, :, pl.ds(n * COLS, COLS)] = coeff_wide[:, k, :]
    column = lax.broadcasted_iota(I32, (EXTENT, COLS), 0)

    def hot_rows(step, _):
        n, pair = step // 8, lax.rem(step, 8)
        for u in range(4):
            r = pair * 4 + u
            at = corner[n, pl.ds(r, 1), :]
            start = at - ((at * 23832) >> 22) * EXTENT
            hot[n, pair // 2, :, pl.ds(pl.multiple_of((lax.rem(pair, 2) * 4 + u) * COLS, COLS), COLS)] = jnp.where(
                column == start, 1.0, 0.0
            ).astype(BF16)
        return 0

    lax.fori_loop(0, ITEMS * 8, hot_rows, 0)


def warp(me, tiles, corner, weight, region, sides, warped):
    lane = lax.broadcasted_iota(I32, (ROWS, COLS), 1)
    for t in range(3):
        left = region[t, pl.ds(PAD, ROWS), :]
        right = region[t + 2, pl.ds(PAD, ROWS), :]
        if t < 2:
            left = jnp.where(me - 2 + t >= 0, left, 0.0)
        if t > 0:
            right = jnp.where(me + t <= lax.axis_size("tile") - 1, right, 0.0)
        sides[t, pl.ds(PAD, ROWS), :] = jnp.where(lane >= COLS // 2, left, right)

    def one(step, _):
        n, block = step // 4, lax.rem(step, 4)
        r0 = pl.multiple_of(block * 8, 8)
        t = jnp.clip(tiles[n] - (me - 1), 0, 2)
        at = corner[n, pl.ds(r0, 8), :]
        q = (at * 23832) >> 22
        p = at - q * EXTENT
        rel = q - (lax.broadcasted_iota(I32, (8, COLS), 0) + r0) + 3
        total = jnp.zeros((8, COLS), F32)
        for dp in range(2):
            index = (p + (dp + COLS - MARGIN)) & (COLS - 1)
            middle = (p + dp >= MARGIN) & (p + dp < MARGIN + COLS)
            upper = jnp.zeros((8, COLS), F32)
            lower = jnp.zeros((8, COLS), F32)
            for o in range(8):
                rows = pl.ds(r0 + (PAD - 3 + o), 8)
                inside = jnp.take_along_axis(region[t + 1, rows, :], index, axis=1)
                beside = jnp.take_along_axis(sides[t, rows, :], index, axis=1)
                found = jnp.where(middle, inside, beside)
                if o < 7:
                    upper = jnp.where(rel == o, found, upper)
                if o > 0:
                    lower = jnp.where(rel == o - 1, found, lower)
            total += weight[n, dp, pl.ds(r0, 8), :].astype(F32) * upper
            total += weight[n, 2 + dp, pl.ds(r0, 8), :].astype(F32) * lower
        warped[n, pl.ds(r0, 8), :] = total
        return 0

    lax.fori_loop(0, ITEMS * 4, one, 0)


def blur_and_back(obs, ivar, warped, lifted, blur_left, blur_right, coeff_f, misfit_parts, spread, backward):
    lane = lax.broadcasted_iota(I32, (ROWS, COLS), 1)

    def lift(b, _):
        shift = lax.rem(HALF - b + COLS, COLS)
        source = lane + (b - HALF)
        inside = (source >= 0) & (source < COLS)
        at = pl.multiple_of(b * ROWS, ROWS)
        for n in range(ITEMS):
            value = jnp.where(inside, pltpu.roll(warped[n], shift, 1), 0.0)
            high, low = split(value)
            lifted[pl.ds(at, ROWS), pl.ds(n * COLS, COLS)] = high
            lifted[pl.ds(at, ROWS), pl.ds(WIDE + n * COLS, COLS)] = low
        return 0

    lax.fori_loop(0, TAPS, lift, 0)
    both = jnp.dot(blur_left[:, pl.ds(0, DEPTH)], lifted[...], preferred_element_type=F32)
    blurred = both[:, :WIDE] + both[:, WIDE:]
    predicted = jnp.zeros((ROWS, WIDE), F32)
    for k in range(NPSF):
        predicted += coeff_f[k] * blurred[k * ROWS : (k + 1) * ROWS]
    misfit = []
    for n in range(ITEMS):
        misfit.append(
            ivar[n].astype(F32) * (predicted[:, n * COLS : (n + 1) * COLS] - obs[n].astype(F32))
        )
    misfit = jnp.concatenate(misfit, axis=1)
    for k in range(NPSF):
        high, low = split(coeff_f[k] * misfit)
        misfit_parts[pl.ds(k * ROWS, ROWS), pl.ds(0, WIDE)] = high
        misfit_parts[pl.ds(k * ROWS, ROWS), pl.ds(WIDE, WIDE)] = low
    spread[...] = jnp.dot(blur_right[pl.ds(0, DEPTH), :], misfit_parts[...], preferred_element_type=F32)

    def lower(b, sums):
        shift = lax.rem(b - HALF + COLS, COLS)
        source = lane - (b - HALF)
        inside = (source >= 0) & (source < COLS)
        at = pl.multiple_of(b * ROWS, ROWS)
        out = []
        for n in range(ITEMS):
            value = spread[pl.ds(at, ROWS), pl.ds(n * COLS, COLS)]
            value += spread[pl.ds(at, ROWS), pl.ds(WIDE + n * COLS, COLS)]
            out.append(sums[n] + jnp.where(inside, pltpu.roll(value, shift, 1), 0.0))
        return tuple(out)

    zero = jnp.zeros((ROWS, COLS), F32)
    sums = lax.fori_loop(0, TAPS, lower, (zero,) * ITEMS)
    for n in range(ITEMS):
        backward[n] = sums[n]


def scatter(me, tiles, corner, weight, backward, hot, window_grad, gradient):
    window_grad[...] = jnp.zeros_like(window_grad)

    def one(step, _):
        n, block = step // 4, lax.rem(step, 4)
        r0 = pl.multiple_of(block * 8, 8)
        q = ((corner[n, pl.ds(r0, 8), :] * 23832) >> 22) - (r0 - 4)
        parts = []
        for j in range(4):
            value = weight[n, j, pl.ds(r0, 8), :].astype(F32) * backward[n, pl.ds(r0, 8), :]
            high = value.astype(BF16).astype(F32)
            parts.append((high, value - high))
        target = lax.broadcasted_iota(I32, (16, COLS), 0)
        columns = []
        for u in range(8):
            row = jnp.broadcast_to(q[u : u + 1], (16, COLS))
            first, second = target == row, target == row + 1
            stack = []
            for dp in range(2):
                for half in range(2):
                    one_up = jnp.broadcast_to(parts[dp][half][u : u + 1], (16, COLS))
                    one_low = jnp.broadcast_to(parts[2 + dp][half][u : u + 1], (16, COLS))
                    stack.append(jnp.where(first, one_up, jnp.where(second, one_low, 0.0)).astype(BF16))
            columns.append(jnp.concatenate(stack, axis=0))
        values = jnp.concatenate(columns, axis=1)
        found = nt_dot(values, hot[n, block])
        for dp in range(2):
            part = found[dp * 32 : dp * 32 + 16] + found[dp * 32 + 16 : dp * 32 + 32]
            window_grad[n, dp, pl.ds(r0, 16), pl.ds(0, EXTENT)] += part
        return 0

    lax.fori_loop(0, ITEMS * 4, one, 0)
    lane = lax.broadcasted_iota(I32, (ROWS, COLS), 1)
    left_lanes = lane >= COLS // 2
    totals = [jnp.zeros((ROWS, COLS), F32) for _ in range(5)]
    for n in range(ITEMS):
        t = jnp.clip(tiles[n] - (me - 1), 0, 2)
        whole = pltpu.roll(window_grad[n, 0, pl.ds(4, ROWS), :], COLS - MARGIN, 1)
        whole += pltpu.roll(window_grad[n, 1, pl.ds(4, ROWS), :], COLS - MARGIN + 1, 1)
        beside, inside = whole[:, :COLS], whole[:, COLS:]
        left = jnp.where(left_lanes, beside, 0.0)
        right = jnp.where(left_lanes, 0.0, beside)
        for s in range(5):
            if n == 0 and s not in (1, 2, 3):
                continue
            if s - 1 in (0, 1, 2):
                totals[s] += jnp.where(t == s - 1, inside, 0.0)
            if s in (0, 1, 2):
                totals[s] += jnp.where(t == s, left, 0.0)
            if s - 2 in (0, 1, 2):
                totals[s] += jnp.where(t == s - 2, right, 0.0)
    for s in range(5):
        gradient[s] = totals[s]


def kernel(tiles, sky, psf, corner, weight, coeff, obs, ivar, out,
           region, arrived, groups, sides, tap_rows, tap_cols, blur_left, blur_right, coeff_wide, coeff_f,
           hot, warped, lifted, misfit_parts, spread, backward, window_grad, gradient,
           near_send, near_recv, back_send, back_recv, grp_send, grp_recv):
    me, grp = lax.axis_index("tile"), lax.axis_index("grp")
    count, group_count = lax.axis_size("tile"), lax.axis_size("grp")

    def tile_at(offset):
        return lax.rem(me + offset + count, count)

    barrier = pltpu.get_barrier_semaphore()
    for offset in OFFSETS:
        pl.semaphore_signal(barrier, inc=1, device_id=(grp, tile_at(offset)), device_id_type=pl.DeviceIdType.MESH)
    for step in range(1, group_count):
        pl.semaphore_signal(
            barrier, inc=1, device_id=(lax.rem(grp + step, group_count), me), device_id_type=pl.DeviceIdType.MESH
        )
    pl.semaphore_wait(barrier, 4 + group_count - 1)

    near = []
    for number, offset in enumerate(OFFSETS):
        copy = pltpu.make_async_remote_copy(
            src_ref=sky,
            dst_ref=region.at[SLOT[-offset], pl.ds(PAD, ROWS), :],
            send_sem=near_send.at[number],
            recv_sem=near_recv.at[number],
            device_id=(grp, tile_at(offset)),
            device_id_type=pl.DeviceIdType.MESH,
        )
        copy.start()
        near.append(copy)
    region[2, pl.ds(PAD, ROWS), :] = sky[...]
    prepare(psf, corner, coeff, tap_rows, tap_cols, blur_left, blur_right, coeff_wide, coeff_f, hot)
    for copy in near:
        copy.wait()
    warp(me, tiles, corner, weight, region, sides, warped)
    blur_and_back(obs, ivar, warped, lifted, blur_left, blur_right, coeff_f, misfit_parts, spread, backward)
    scatter(me, tiles, corner, weight, backward, hot, window_grad, gradient)

    back = []
    for number, offset in enumerate(OFFSETS):
        copy = pltpu.make_async_remote_copy(
            src_ref=gradient.at[SLOT[offset]],
            dst_ref=arrived.at[number],
            send_sem=back_send.at[number],
            recv_sem=back_recv.at[number],
            device_id=(grp, tile_at(offset)),
            device_id_type=pl.DeviceIdType.MESH,
        )
        copy.start()
        back.append(copy)
    owned = gradient[2]
    for number, offset in enumerate(OFFSETS):
        back[number].wait()
        valid = (me - offset >= 0) & (me - offset <= count - 1)
        owned += jnp.where(valid, arrived[number], 0.0)
    groups[grp] = owned
    sums = []
    for step in range(1, group_count):
        copy = pltpu.make_async_remote_copy(
            src_ref=groups.at[grp],
            dst_ref=groups.at[grp],
            send_sem=grp_send.at[step - 1],
            recv_sem=grp_recv.at[step - 1],
            device_id=(lax.rem(grp + step, group_count), me),
            device_id_type=pl.DeviceIdType.MESH,
        )
        copy.start()
        sums.append(copy)
    for copy in sums:
        copy.wait()
    total = groups[0]
    for g in range(1, group_count):
        total += groups[g]
    out[...] = sky[...] - STEP * total


def per_device(sky, psf_basis, item_tile, warp_corner, warp_weight, psf_coeff, observed, inv_var):
    group_count = lax.axis_size("grp")
    vmem = pl.BlockSpec(memory_space=pltpu.VMEM)
    dma = pltpu.SemaphoreType.DMA
    return pl.pallas_call(
        kernel,
        out_shape=jax.ShapeDtypeStruct((ROWS, COLS), F32),
        in_specs=[pl.BlockSpec(memory_space=pltpu.SMEM)] + [vmem] * 7,
        out_specs=vmem,
        scratch_shapes=[
            pltpu.VMEM((5, ROWS + 2 * PAD, COLS), F32),
            pltpu.VMEM((4, ROWS, COLS), F32),
            pltpu.VMEM((group_count, ROWS, COLS), F32),
            pltpu.VMEM((3, ROWS + 2 * PAD, COLS), F32),
            pltpu.VMEM((NPSF, COLS, COLS), F32),
            pltpu.VMEM((NPSF, COLS, COLS), F32),
            pltpu.VMEM((NPSF * ROWS, GROUPS_OF_4 * COLS), BF16),
            pltpu.VMEM((GROUPS_OF_4 * COLS, NPSF * ROWS), BF16),
            pltpu.VMEM((ROWS, 8, COLS), F32),
            pltpu.VMEM((NPSF, ROWS, WIDE), F32),
            pltpu.VMEM((ITEMS, 4, EXTENT, 8 * COLS), BF16),
            pltpu.VMEM((ITEMS, ROWS, COLS), F32),
            pltpu.VMEM((DEPTH, 2 * WIDE), BF16),
            pltpu.VMEM((NPSF * ROWS, 2 * WIDE), BF16),
            pltpu.VMEM((DEPTH, 2 * WIDE), F32),
            pltpu.VMEM((ITEMS, ROWS, COLS), F32),
            pltpu.VMEM((ITEMS, 2, ROWS + 8, 2 * COLS), F32),
            pltpu.VMEM((5, ROWS, COLS), F32),
            dma((4,)), dma((4,)), dma((4,)), dma((4,)), dma((group_count - 1,)), dma((group_count - 1,)),
        ],
        compiler_params=pltpu.CompilerParams(
            collective_id=0, has_side_effects=True, vmem_limit_bytes=48 * 2**20
        ),
    )(item_tile, sky, psf_basis, warp_corner, warp_weight, psf_coeff, observed, inv_var)


def solution(mesh):
    return jax.shard_map(
        per_device,
        mesh=mesh,
        in_specs=(
            P(None, "tile"),
            P("grp", None, None, None),
            P(("grp", "tile")),
            P(("grp", "tile"), None, None),
            P(("grp", "tile"), None, None, None),
            P(("grp", "tile"), None, None, None),
            P(("grp", "tile"), None, None),
            P(("grp", "tile"), None, None),
        ),
        out_specs=P(None, "tile"),
        check_vma=False,
    )
```

time: 355 us -> 41 us (0.12)
  the two profiles are of different devices: /device:TPU:129 before, /device:TPU:1 now
where the time goes in v1:
time: 41 us; the launch traced here: 40.9 us
  Pallas kernels  39.1 us (95%)
  local copies, waits for them, and re-layouts  1.71 us (4%)
    pallas_call x1, Pallas kernels, per_device(): pl.pallas_call(kernel, out_shape=jax.ShapeDtypeStruct((ROWS, COLS), F32),...  39.1 us
    unnamed x16, local copies, waits for them, and re-layouts  1.71 us

profile of v1, /device:TPU:1, one launch (start us, length us, event | category | flops | bytes accessed | tf_op | source)
XLA Modules:
  0.0 40.9 jit_solution(17364184003058149807)
XLA Ops:
  0.0 0.0 copy-start.4
  0.0 0.0 copy-start.3
  0.0 0.0 copy-start
  0.0 0.0 copy-start.2
  0.0 0.0 copy-start.6
  0.0 0.0 copy-start.1
  0.0 0.0 copy-start.5
  0.0 1.1 %copy.9.coeff = bf16[3,32,5,128]{3,2,1,0:T(8,128)(2,1)S(1)} copy(bf16[3,32,5,128]{3,1,2,0:T(8,128)(2,1)} %param.13) | data formatting | bytes 245760 | tf_op args[5]
  1.1 0.0 copy-done.4
  1.1 0.0 copy-done.3
  1.1 0.0 copy-done
  1.2 0.0 copy-done.2
  1.2 0.0 copy-done.6
  1.2 0.0 copy-done.1
  1.2 0.0 copy-done.5
  1.2 39.1 %shard_map.82 = f32[32,128]{1,0:T(8,128)S(1)} custom-call(s32[3]{0:T(128)S(1)} %copy-done.6, f32[32,128]{1,0:T(8,128)S(1)} %copy-done.5, bf16[1,5,41,41]{3,2,1,0:T(8,128)(2,1)S(1)} %copy-done.1, s32[3,32,128]{2,1,0:T(8,128)S(1)} %copy-done.2, bf16[3,4,32,128]{3,2,1,0:T(8,128)(2,1)S(1)} %copy-done, bf16[3,32,5,128]{3,2,1,0:T(8,128)(2,1)S(1)} %copy.9.coeff, ...), custom_call_target="tpu_custom_call" | custom-call | tf_op jit(solution)/shard_map/pallas_call | solution.py:306
  40.3 0.6 %copy.11 = f32[32,128]{1,0:T(8,128)} copy(f32[32,128]{1,0:T(8,128)S(1)} %shard_map.82) | data formatting | bytes 32768
Async XLA Ops:
  0.0 1.1 %copy-start.4 = (bf16[3,32,128]{2,1,0:T(8,128)(2,1)S(1)}, bf16[3,32,128]{2,1,0:T(8,128)(2,1)}, u32[]{:S(2)}) copy-start(bf16[3,32,128]{2,1,0:T(8,128)(2,1)} %ivar.1) | copy-start | bytes 73732
  0.0 1.1 %copy-start.3 = (bf16[3,32,128]{2,1,0:T(8,128)(2,1)S(1)}, bf16[3,32,128]{2,1,0:T(8,128)(2,1)}, u32[]{:S(2)}) copy-start(bf16[3,32,128]{2,1,0:T(8,128)(2,1)} %obs.1) | copy-start | bytes 73732
  0.0 1.1 %copy-start = (bf16[3,4,32,128]{3,2,1,0:T(8,128)(2,1)S(1)}, bf16[3,4,32,128]{3,2,1,0:T(8,128)(2,1)}, u32[]{:S(2)}) copy-start(bf16[3,4,32,128]{3,2,1,0:T(8,128)(2,1)} %weight.1) | copy-start | bytes 294916
  0.0 1.1 %copy-start.2 = (s32[3,32,128]{2,1,0:T(8,128)S(1)}, s32[3,32,128]{2,1,0:T(8,128)}, u32[]{:S(2)}) copy-start(s32[3,32,128]{2,1,0:T(8,128)} %corner.1) | copy-start | bytes 147460
  0.0 1.1 %copy-start.6 = (s32[3]{0:T(128)S(1)}, s32[3]{0:T(128)}, u32[]{:S(2)}) copy-start(s32[3]{0:T(128)} %tiles.1) | copy-start | bytes 40
  0.0 1.1 %copy-start.1 = (bf16[1,5,41,41]{3,2,1,0:T(8,128)(2,1)S(1)}, bf16[1,5,41,41]{3,2,1,0:T(8,128)(2,1)}, u32[]{:S(2)}) copy-start(bf16[1,5,41,41]{3,2,1,0:T(8,128)(2,1)} %psf.1) | copy-start | bytes 50434
  0.0 1.1 %copy-start.5 = (f32[32,128]{1,0:T(8,128)S(1)}, f32[32,128]{1,0:T(8,128)}, u32[]{:S(2)}) copy-start(f32[32,128]{1,0:T(8,128)} %sky.1) | copy-start | bytes 49156

commit v2 on v1

v2 whole, which is shorter than its diff:
```python
import functools

import jax
import jax.numpy as jnp
from jax import lax
from jax.experimental import pallas as pl
from jax.experimental.pallas import tpu as pltpu
from jax.sharding import PartitionSpec as P

F32, BF16, I32 = jnp.float32, jnp.bfloat16, jnp.int32
ROWS, COLS, MARGIN, TAPS, NPSF, ITEMS = 32, 128, 24, 41, 5, 3
EXTENT = COLS + 2 * MARGIN
HALF = TAPS // 2
WIDE = ITEMS * COLS
DEPTH = TAPS * ROWS
GROUPS_OF_4 = (TAPS + 3) // 4
PAD = 8
STEP = 0.25
OFFSETS = (-2, -1, 1, 2)
SLOT = {-2: 0, -1: 1, 0: 2, 1: 3, 2: 4}


def split(value):
    high = value.astype(BF16)
    return high, (value - high.astype(F32)).astype(BF16)


def nt_dot(a, b):
    return lax.dot_general(a, b, (((1,), (1,)), ((), ())), preferred_element_type=F32)


def prepare_hot(corner, hot):
    column = lax.broadcasted_iota(I32, (EXTENT, COLS), 0)

    def hot_rows(step, _):
        n, block = step // 4, lax.rem(step, 4)
        at = corner[n, pl.ds(pl.multiple_of(block * 8, 8), 8), :]
        start = at - ((at * 23832) >> 22) * EXTENT
        for u in range(8):
            row = jnp.broadcast_to(start[u : u + 1], (EXTENT, COLS))
            hot[n, block, :, pl.ds(u * COLS, COLS)] = jnp.where(column == row, 1.0, 0.0).astype(BF16)
        return 0

    lax.fori_loop(0, ITEMS * 4, hot_rows, 0)


def prepare_taps(psf, tap_rows, tap_cols, blur_left, blur_right):
    tap_rows[...] = jnp.zeros_like(tap_rows)
    for k in range(NPSF):
        tap_rows[k, pl.ds(0, TAPS), pl.ds(0, TAPS)] = psf[0, k].astype(F32)
    for k in range(NPSF):
        tap_cols[k] = pltpu.roll(tap_rows[k], 4, 0).T
    lane_group = lax.broadcasted_iota(I32, (8, COLS), 1) // ROWS
    for j in range(GROUPS_OF_4):
        whole = []
        for k in range(NPSF):
            for r0 in range(0, ROWS, 8):
                tile = jnp.zeros((8, COLS), F32)
                for part in range(4):
                    row = jnp.broadcast_to(tap_cols[k, pl.ds(4 * j + part, 1), :], (8, COLS))
                    turned = pltpu.roll(row, (r0 + ROWS * part - HALF - 4) % COLS, 1, stride=1, stride_axis=0)
                    tile = turned if part == 0 else jnp.where(lane_group == part, turned, tile)
                whole.append(tile)
        whole = jnp.concatenate(whole, axis=0)
        blur_left[:, pl.ds(j * COLS, COLS)] = whole.astype(BF16)
        blur_right[pl.ds(j * COLS, COLS), :] = whole.T.astype(BF16)


def warp(me, count, tiles, corner, weight, region, sides, warped):
    lane = lax.broadcasted_iota(I32, (ROWS, COLS), 1)
    for t in range(3):
        left = region[t, pl.ds(PAD, ROWS), :]
        right = region[t + 2, pl.ds(PAD, ROWS), :]
        if t < 2:
            left = jnp.where(me - 2 + t >= 0, left, 0.0)
        if t > 0:
            right = jnp.where(me + t <= count - 1, right, 0.0)
        sides[t, pl.ds(PAD, ROWS), :] = jnp.where(lane >= COLS // 2, left, right)
    for n in range(ITEMS):
        t = jnp.clip(tiles[n] - (me - 1), 0, 2)
        for r0 in range(0, ROWS, 8):
            at = corner[n, pl.ds(r0, 8), :]
            q = (at * 23832) >> 22
            p = at - q * EXTENT
            rel = q - (lax.broadcasted_iota(I32, (8, COLS), 0) + r0) + 3
            total = jnp.zeros((8, COLS), F32)
            for dp in range(2):
                index = (p + (dp + COLS - MARGIN)) & (COLS - 1)
                middle = (p + dp >= MARGIN) & (p + dp < MARGIN + COLS)
                upper = jnp.zeros((8, COLS), F32)
                lower = jnp.zeros((8, COLS), F32)
                for o in range(8):
                    rows = pl.ds(r0 + (PAD - 3 + o), 8)
                    inside = jnp.take_along_axis(region[t + 1, rows, :], index, axis=1)
                    beside = jnp.take_along_axis(sides[t, rows, :], index, axis=1)
                    found = jnp.where(middle, inside, beside)
                    if o < 7:
                        upper = jnp.where(rel == o, found, upper)
                    if o > 0:
                        lower = jnp.where(rel == o - 1, found, lower)
                total += weight[n, dp, pl.ds(r0, 8), :].astype(F32) * upper
                total += weight[n, 2 + dp, pl.ds(r0, 8), :].astype(F32) * lower
            warped[n, pl.ds(r0, 8), :] = total


def blur(coeff, obs, ivar, warped, lifted, blur_left, misfit_parts):
    lane = lax.broadcasted_iota(I32, (ROWS, COLS), 1)
    for b in range(TAPS):
        source = lane + (b - HALF)
        inside = (source >= 0) & (source < COLS)
        for n in range(ITEMS):
            value = warped[n]
            if b != HALF:
                value = jnp.where(inside, pltpu.roll(value, (HALF - b) % COLS, 1), 0.0)
            high, low = split(value)
            lifted[pl.ds(b * ROWS, ROWS), pl.ds(n * COLS, COLS)] = high
            lifted[pl.ds(b * ROWS, ROWS), pl.ds(WIDE + n * COLS, COLS)] = low
    both = jnp.dot(blur_left[:, pl.ds(0, DEPTH)], lifted[...], preferred_element_type=F32)
    blurred = both[:, :WIDE] + both[:, WIDE:]
    for n in range(ITEMS):
        predicted = jnp.zeros((ROWS, COLS), F32)
        for k in range(NPSF):
            predicted += coeff[n, k].astype(F32) * blurred[k * ROWS : (k + 1) * ROWS, n * COLS : (n + 1) * COLS]
        misfit = ivar[n].astype(F32) * (predicted - obs[n].astype(F32))
        for k in range(NPSF):
            high, low = split(coeff[n, k].astype(F32) * misfit)
            misfit_parts[pl.ds(k * ROWS, ROWS), pl.ds(n * COLS, COLS)] = high
            misfit_parts[pl.ds(k * ROWS, ROWS), pl.ds(WIDE + n * COLS, COLS)] = low


def back(blur_right, misfit_parts, spread, backward):
    lane = lax.broadcasted_iota(I32, (ROWS, COLS), 1)
    spread[...] = jnp.dot(blur_right[pl.ds(0, DEPTH), :], misfit_parts[...], preferred_element_type=F32)
    for n in range(ITEMS):
        total = jnp.zeros((ROWS, COLS), F32)
        for b in range(TAPS):
            source = lane - (b - HALF)
            inside = (source >= 0) & (source < COLS)
            value = spread[pl.ds(b * ROWS, ROWS), pl.ds(n * COLS, COLS)]
            value += spread[pl.ds(b * ROWS, ROWS), pl.ds(WIDE + n * COLS, COLS)]
            if b != HALF:
                value = jnp.where(inside, pltpu.roll(value, (b - HALF) % COLS, 1), 0.0)
            total += value
        backward[n] = total


def scatter(corner, weight, backward, hot, parts, window_grad):
    window_grad[...] = jnp.zeros_like(window_grad)
    target = lax.broadcasted_iota(I32, (16, COLS), 0)
    for n in range(ITEMS):
        for j in range(4):
            value = weight[n, j].astype(F32) * backward[n]
            high = value.astype(BF16).astype(F32)
            parts[n, j, 0] = high
            parts[n, j, 1] = value - high
        for block in range(4):
            r0 = block * 8
            q = ((corner[n, pl.ds(r0, 8), :] * 23832) >> 22) - (r0 - 4)
            columns = []
            for u in range(8):
                row = jnp.broadcast_to(q[u : u + 1], (16, COLS))
                first, second = target == row, target == row + 1
                stack = []
                for dp in range(2):
                    for half in range(2):
                        one_up = jnp.broadcast_to(parts[n, dp, half, pl.ds(r0 + u, 1), :], (16, COLS))
                        one_low = jnp.broadcast_to(parts[n, 2 + dp, half, pl.ds(r0 + u, 1), :], (16, COLS))
                        stack.append(jnp.where(first, one_up, jnp.where(second, one_low, 0.0)).astype(BF16))
                columns.append(jnp.concatenate(stack, axis=0))
            values = jnp.concatenate(columns, axis=1)
            found = nt_dot(values, hot[n, block])
            for dp in range(2):
                part = found[dp * 32 : dp * 32 + 16] + found[dp * 32 + 16 : dp * 32 + 32]
                window_grad[n, dp, pl.ds(r0, 16), pl.ds(0, EXTENT)] += part


def gather_tiles(me, tiles, window_grad, gradient):
    lane = lax.broadcasted_iota(I32, (ROWS, COLS), 1)
    left_lanes = lane >= COLS // 2
    totals = [jnp.zeros((ROWS, COLS), F32) for _ in range(5)]
    for n in range(ITEMS):
        t = jnp.clip(tiles[n] - (me - 1), 0, 2)
        whole = pltpu.roll(window_grad[n, 0, pl.ds(4, ROWS), :], COLS - MARGIN, 1)
        whole += pltpu.roll(window_grad[n, 1, pl.ds(4, ROWS), :], COLS - MARGIN + 1, 1)
        beside, inside = whole[:, :COLS], whole[:, COLS:]
        left = jnp.where(left_lanes, beside, 0.0)
        right = jnp.where(left_lanes, 0.0, beside)
        for s in range(5):
            if n == 0 and s not in (1, 2, 3):
                continue
            if s - 1 in (0, 1, 2):
                totals[s] += jnp.where(t == s - 1, inside, 0.0)
            if s in (0, 1, 2):
                totals[s] += jnp.where(t == s, left, 0.0)
            if s - 2 in (0, 1, 2):
                totals[s] += jnp.where(t == s - 2, right, 0.0)
    for s in range(5):
        gradient[s] = totals[s]


def kernel(tiles, sky_hbm, psf, corner_hbm, weight_hbm, coeff_hbm, obs_hbm, ivar_hbm, out,
           corner, weight, coeff, obs, ivar,
           region, arrived, groups, sides, tap_rows, tap_cols, blur_left, blur_right,
           hot, warped, lifted, misfit_parts, spread, backward, parts, window_grad, gradient,
           load, near_send, near_recv, back_send, back_recv, grp_send, grp_recv):
    me, grp = lax.axis_index("tile"), lax.axis_index("grp")
    count, group_count = lax.axis_size("tile"), lax.axis_size("grp")
    mesh_id = pl.DeviceIdType.MESH
    there = {offset: (me + offset >= 0) & (me + offset <= count - 1) for offset in OFFSETS}
    barrier = pltpu.get_barrier_semaphore()
    for offset in OFFSETS:
        @pl.when(there[offset])
        def _():
            pl.semaphore_signal(barrier, inc=1, device_id=(grp, me + offset), device_id_type=mesh_id)
    for step in range(1, group_count):
        other = lax.rem(grp + step, group_count)
        pl.semaphore_signal(barrier, inc=1, device_id=(other, me), device_id_type=mesh_id)
    sky_here = region.at[2, pl.ds(PAD, ROWS), :]
    pairs = ((corner_hbm, corner), (sky_hbm, sky_here), (weight_hbm, weight),
             (coeff_hbm, coeff), (obs_hbm, obs), (ivar_hbm, ivar))
    loads = [pltpu.make_async_copy(a, b, load.at[i]) for i, (a, b) in enumerate(pairs)]
    for copy in loads:
        copy.start()
    loads[0].wait()
    prepare_hot(corner, hot)
    pl.semaphore_wait(barrier, jnp.minimum(me, 2) + jnp.minimum(count - 1 - me, 2) + group_count - 1)

    near = []
    for number, offset in enumerate(OFFSETS):
        near.append(pltpu.make_async_remote_copy(
            src_ref=sky_hbm,
            dst_ref=region.at[SLOT[-offset], pl.ds(PAD, ROWS), :],
            send_sem=near_send.at[number],
            recv_sem=near_recv.at[number],
            device_id=(grp, me + offset),
            device_id_type=mesh_id,
        ))
        pl.when(there[offset])(near[number].start)
    prepare_taps(psf, tap_rows, tap_cols, blur_left, blur_right)
    for copy in loads[1:]:
        copy.wait()
    for number, offset in enumerate(OFFSETS):
        pl.when(there[-offset])(near[number].wait_recv)
    warp(me, count, tiles, corner, weight, region, sides, warped)
    blur(coeff, obs, ivar, warped, lifted, blur_left, misfit_parts)
    back(blur_right, misfit_parts, spread, backward)
    scatter(corner, weight, backward, hot, parts, window_grad)
    gather_tiles(me, tiles, window_grad, gradient)

    home = []
    for number, offset in enumerate(OFFSETS):
        home.append(pltpu.make_async_remote_copy(
            src_ref=gradient.at[SLOT[offset]],
            dst_ref=arrived.at[number],
            send_sem=back_send.at[number],
            recv_sem=back_recv.at[number],
            device_id=(grp, me + offset),
            device_id_type=mesh_id,
        ))
        pl.when(there[offset])(home[number].start)
    owned = gradient[2]
    for number, offset in enumerate(OFFSETS):
        pl.when(there[-offset])(home[number].wait_recv)
        owned += jnp.where(there[-offset], arrived[number], 0.0)
    groups[grp] = owned
    sums = []
    for step in range(1, group_count):
        sums.append(pltpu.make_async_remote_copy(
            src_ref=groups.at[grp],
            dst_ref=groups.at[grp],
            send_sem=grp_send.at[step - 1],
            recv_sem=grp_recv.at[step - 1],
            device_id=(lax.rem(grp + step, group_count), me),
            device_id_type=mesh_id,
        ))
        sums[-1].start()
    for number, offset in enumerate(OFFSETS):
        pl.when(there[offset])(near[number].wait_send)
        pl.when(there[offset])(home[number].wait_send)
    for copy in sums:
        copy.wait()
    total = groups[0]
    for g in range(1, group_count):
        total += groups[g]
    out[...] = region[2, pl.ds(PAD, ROWS), :] - STEP * total


def per_device(sky, psf_basis, item_tile, warp_corner, warp_weight, psf_coeff, observed, inv_var):
    group_count = lax.axis_size("grp")
    vmem = pl.BlockSpec(memory_space=pltpu.VMEM)
    dma = pltpu.SemaphoreType.DMA
    hbm = pl.BlockSpec(memory_space=pltpu.HBM)
    coeff = psf_coeff.transpose(0, 2, 1, 3)
    return pl.pallas_call(
        kernel,
        out_shape=jax.ShapeDtypeStruct((ROWS, COLS), F32),
        in_specs=[pl.BlockSpec(memory_space=pltpu.SMEM), hbm, vmem] + [hbm] * 5,
        out_specs=vmem,
        scratch_shapes=[
            pltpu.VMEM(warp_corner.shape, I32),
            pltpu.VMEM(warp_weight.shape, BF16),
            pltpu.VMEM(coeff.shape, BF16),
            pltpu.VMEM(observed.shape, BF16),
            pltpu.VMEM(inv_var.shape, BF16),
            pltpu.VMEM((5, ROWS + 2 * PAD, COLS), F32),
            pltpu.VMEM((4, ROWS, COLS), F32),
            pltpu.VMEM((group_count, ROWS, COLS), F32),
            pltpu.VMEM((3, ROWS + 2 * PAD, COLS), F32),
            pltpu.VMEM((NPSF, COLS, COLS), F32),
            pltpu.VMEM((NPSF, COLS, COLS), F32),
            pltpu.VMEM((NPSF * ROWS, GROUPS_OF_4 * COLS), BF16),
            pltpu.VMEM((GROUPS_OF_4 * COLS, NPSF * ROWS), BF16),
            pltpu.VMEM((ITEMS, 4, EXTENT, 8 * COLS), BF16),
            pltpu.VMEM((ITEMS, ROWS, COLS), F32),
            pltpu.VMEM((DEPTH, 2 * WIDE), BF16),
            pltpu.VMEM((NPSF * ROWS, 2 * WIDE), BF16),
            pltpu.VMEM((DEPTH, 2 * WIDE), F32),
            pltpu.VMEM((ITEMS, ROWS, COLS), F32),
            pltpu.VMEM((ITEMS, 4, 2, ROWS, COLS), F32),
            pltpu.VMEM((ITEMS, 2, ROWS + 8, 2 * COLS), F32),
            pltpu.VMEM((5, ROWS, COLS), F32),
            dma((6,)), dma((4,)), dma((4,)), dma((4,)), dma((4,)), dma((group_count - 1,)), dma((group_count - 1,)),
        ],
        compiler_params=pltpu.CompilerParams(
            collective_id=0, has_side_effects=True, vmem_limit_bytes=62 * 2**20
        ),
    )(item_tile, sky, psf_basis, warp_corner, warp_weight, coeff, observed, inv_var)


def solution(mesh):
    return jax.shard_map(
        per_device,
        mesh=mesh,
        in_specs=(
            P(None, "tile"),
            P("grp", None, None, None),
            P(("grp", "tile")),
            P(("grp", "tile"), None, None),
            P(("grp", "tile"), None, None, None),
            P(("grp", "tile"), None, None, None),
            P(("grp", "tile"), None, None),
            P(("grp", "tile"), None, None),
        ),
        out_specs=P(None, "tile"),
        check_vma=False,
    )
```

time: 41 us -> 26.1 us (0.64)
  the two profiles are of different devices: /device:TPU:1 before, /device:TPU:129 now
where the time goes in v2:
time: 26.1 us; the launch traced here: 25.9 us
  Pallas kernels  24.6 us (94%)
  local copies, waits for them, and re-layouts  1.32 us (5%)
    pallas_call x1, Pallas kernels, per_device(): pl.pallas_call(kernel, out_shape=jax.ShapeDtypeStruct((ROWS, COLS), F32),...  24.6 us
    unnamed x1, local copies, waits for them, and re-layouts  1.32 us

profile of v2, /device:TPU:129, one launch (start us, length us, event | category | flops | bytes accessed | tf_op | source)
XLA Modules:
  0.0 25.9 jit_solution(2761106005127345574)
XLA Ops:
  0.0 24.6 %shard_map.82 = f32[32,128]{1,0:T(8,128)} custom-call(s32[3]{0:T(128)} %tiles.1, f32[32,128]{1,0:T(8,128)} %sky_hbm.1, bf16[1,5,41,41]{3,2,1,0:T(8,128)(2,1)} %psf.1, s32[3,32,128]{2,1,0:T(8,128)} %corner_hbm.1, bf16[3,4,32,128]{3,2,1,0:T(8,128)(2,1)} %weight_hbm.1, bf16[3,5,32,128]{3,2,1,0:T(8,128)(2,1)} %bitcast.1, bf16[3,32,128]{2,1,0:T(8,128)(2,1)} %obs_hbm.1, ...), custom_call_target="tpu_custom_call" | custom-call | tf_op jit(solution)/shard_map/pallas_call | solution.py:294
  24.6 1.3 %copy.10 = f32[32,128]{1,0:T(8,128)} copy(f32[32,128]{1,0:T(8,128)} %shard_map.82) | data formatting | bytes 32768

commit v3 on v2

--- a/solution.py
+++ b/solution.py
@@ -27,6 +27,21 @@
 
 def nt_dot(a, b):
     return lax.dot_general(a, b, (((1,), (1,)), ((), ())), preferred_element_type=F32)
+
+
+def pack(value, right):
+    lane_group = lax.broadcasted_iota(I32, (8, COLS), 1) // ROWS
+    packed = jnp.zeros((8, COLS), F32)
+    for i in range(4):
+        turned = pltpu.roll(value[8 * i : 8 * i + 8], (32 * i + (ROWS if right else 0)) % COLS, 1)
+        packed = jnp.where(lane_group == i, turned, packed)
+    return packed
+
+
+def unpack(packed, right):
+    return jnp.concatenate(
+        [pltpu.roll(packed, (-32 * i - (ROWS if right else 0)) % COLS, 1) for i in range(4)], axis=0
+    )
 
 
 def prepare_hot(corner, hot):
@@ -66,11 +81,11 @@
         blur_right[pl.ds(j * COLS, COLS), :] = whole.T.astype(BF16)
 
 
-def warp(me, count, tiles, corner, weight, region, sides, warped):
+def warp(me, count, tiles, corner, weight, region, far_in, sides, warped):
     lane = lax.broadcasted_iota(I32, (ROWS, COLS), 1)
     for t in range(3):
-        left = region[t, pl.ds(PAD, ROWS), :]
-        right = region[t + 2, pl.ds(PAD, ROWS), :]
+        left = unpack(far_in[1], True) if t == 0 else region[t, pl.ds(PAD, ROWS), :]
+        right = unpack(far_in[0], False) if t == 2 else region[t + 2, pl.ds(PAD, ROWS), :]
         if t < 2:
             left = jnp.where(me - 2 + t >= 0, left, 0.0)
         if t > 0:
@@ -174,7 +189,7 @@
                 window_grad[n, dp, pl.ds(r0, 16), pl.ds(0, EXTENT)] += part
 
 
-def gather_tiles(me, tiles, window_grad, gradient):
+def gather_tiles(me, tiles, window_grad, gradient, far_gradient):
     lane = lax.broadcasted_iota(I32, (ROWS, COLS), 1)
     left_lanes = lane >= COLS // 2
     totals = [jnp.zeros((ROWS, COLS), F32) for _ in range(5)]
@@ -194,95 +209,113 @@
                 totals[s] += jnp.where(t == s, left, 0.0)
             if s - 2 in (0, 1, 2):
                 totals[s] += jnp.where(t == s - 2, right, 0.0)
-    for s in range(5):
-        gradient[s] = totals[s]
+    for s in range(3):
+        gradient[s] = totals[s + 1]
+    far_gradient[0] = pack(totals[0], True)
+    far_gradient[1] = pack(totals[4], False)
 
 
 def kernel(tiles, sky_hbm, psf, corner_hbm, weight_hbm, coeff_hbm, obs_hbm, ivar_hbm, out,
            corner, weight, coeff, obs, ivar,
-           region, arrived, groups, sides, tap_rows, tap_cols, blur_left, blur_right,
-           hot, warped, lifted, misfit_parts, spread, backward, parts, window_grad, gradient,
-           load, near_send, near_recv, back_send, back_recv, grp_send, grp_recv):
+           region, far_out, far_in, arrived, far_arrived, sides, tap_rows, tap_cols, blur_left, blur_right,
+           hot, warped, lifted, misfit_parts, spread, backward, parts, window_grad, gradient, far_gradient,
+           load, near_send, near_recv, back_send, back_recv):
     me, grp = lax.axis_index("tile"), lax.axis_index("grp")
     count, group_count = lax.axis_size("tile"), lax.axis_size("grp")
     mesh_id = pl.DeviceIdType.MESH
     there = {offset: (me + offset >= 0) & (me + offset <= count - 1) for offset in OFFSETS}
+    others = [lax.rem(grp + step, group_count) for step in range(group_count)]
     barrier = pltpu.get_barrier_semaphore()
-    for offset in OFFSETS:
-        @pl.when(there[offset])
-        def _():
-            pl.semaphore_signal(barrier, inc=1, device_id=(grp, me + offset), device_id_type=mesh_id)
-    for step in range(1, group_count):
-        other = lax.rem(grp + step, group_count)
-        pl.semaphore_signal(barrier, inc=1, device_id=(other, me), device_id_type=mesh_id)
+    for step in range(group_count):
+        for offset in OFFSETS:
+            @pl.when(there[offset])
+            def _():
+                pl.semaphore_signal(barrier, inc=1, device_id=(others[step], me + offset), device_id_type=mesh_id)
+        if step > 0:
+            pl.semaphore_signal(barrier, inc=1, device_id=(others[step], me), device_id_type=mesh_id)
     sky_here = region.at[2, pl.ds(PAD, ROWS), :]
-    pairs = ((corner_hbm, corner), (sky_hbm, sky_here), (weight_hbm, weight),
+    pairs = ((sky_hbm, sky_here), (corner_hbm, corner), (weight_hbm, weight),
              (coeff_hbm, coeff), (obs_hbm, obs), (ivar_hbm, ivar))
     loads = [pltpu.make_async_copy(a, b, load.at[i]) for i, (a, b) in enumerate(pairs)]
     for copy in loads:
         copy.start()
     loads[0].wait()
+    far_out[0] = pack(sky_here[...], False)
+    far_out[1] = pack(sky_here[...], True)
+    loads[1].wait()
     prepare_hot(corner, hot)
-    pl.semaphore_wait(barrier, jnp.minimum(me, 2) + jnp.minimum(count - 1 - me, 2) + group_count - 1)
+    neighbours = jnp.minimum(me, 2) + jnp.minimum(count - 1 - me, 2)
+    pl.semaphore_wait(barrier, (neighbours + 1) * group_count - 1)
 
     near = []
     for number, offset in enumerate(OFFSETS):
+        side = 0 if offset < 0 else 1
         near.append(pltpu.make_async_remote_copy(
-            src_ref=sky_hbm,
-            dst_ref=region.at[SLOT[-offset], pl.ds(PAD, ROWS), :],
+            src_ref=sky_here if abs(offset) == 1 else far_out.at[side],
+            dst_ref=region.at[SLOT[-offset], pl.ds(PAD, ROWS), :] if abs(offset) == 1 else far_in.at[side],
             send_sem=near_send.at[number],
             recv_sem=near_recv.at[number],
             device_id=(grp, me + offset),
             device_id_type=mesh_id,
         ))
-        pl.when(there[offset])(near[number].start)
+    for number in (0, 3, 1, 2):
+        pl.when(there[OFFSETS[number]])(near[number].start)
     prepare_taps(psf, tap_rows, tap_cols, blur_left, blur_right)
-    for copy in loads[1:]:
+    for copy in loads[2:]:
         copy.wait()
     for number, offset in enumerate(OFFSETS):
         pl.when(there[-offset])(near[number].wait_recv)
-    warp(me, count, tiles, corner, weight, region, sides, warped)
+    warp(me, count, tiles, corner, weight, region, far_in, sides, warped)
     blur(coeff, obs, ivar, warped, lifted, blur_left, misfit_parts)
     back(blur_right, misfit_parts, spread, backward)
     scatter(corner, weight, backward, hot, parts, window_grad)
-    gather_tiles(me, tiles, window_grad, gradient)
+    gather_tiles(me, tiles, window_grad, gradient, far_gradient)
 
     home = []
-    for number, offset in enumerate(OFFSETS):
-        home.append(pltpu.make_async_remote_copy(
-            src_ref=gradient.at[SLOT[offset]],
-            dst_ref=arrived.at[number],
-            send_sem=back_send.at[number],
-            recv_sem=back_recv.at[number],
-            device_id=(grp, me + offset),
-            device_id_type=mesh_id,
-        ))
-        pl.when(there[offset])(home[number].start)
-    owned = gradient[2]
-    for number, offset in enumerate(OFFSETS):
-        pl.when(there[-offset])(home[number].wait_recv)
-        owned += jnp.where(there[-offset], arrived[number], 0.0)
-    groups[grp] = owned
-    sums = []
-    for step in range(1, group_count):
-        sums.append(pltpu.make_async_remote_copy(
-            src_ref=groups.at[grp],
-            dst_ref=groups.at[grp],
-            send_sem=grp_send.at[step - 1],
-            recv_sem=grp_recv.at[step - 1],
-            device_id=(lax.rem(grp + step, group_count), me),
-            device_id_type=mesh_id,
-        ))
-        sums[-1].start()
+    for offset in (-2, 2, -1, 1, 0):
+        for step in range(group_count):
+            if offset == 0 and step == 0:
+                continue
+            number = OFFSETS.index(offset) if offset else 4
+            if abs(offset) == 2:
+                source, target = far_gradient.at[number // 3], far_arrived.at[grp, number // 3]
+            else:
+                source, target = gradient.at[offset + 1], arrived.at[grp, offset + 1]
+            copy = pltpu.make_async_remote_copy(
+                src_ref=source,
+                dst_ref=target,
+                send_sem=back_send.at[step, number],
+                recv_sem=back_recv.at[step, number],
+                device_id=(others[step], me + offset),
+                device_id_type=mesh_id,
+            )
+            home.append((offset, copy))
+            if offset == 0:
+                copy.start()
+            else:
+                pl.when(there[offset])(copy.start)
+    arrived[grp, 1] = gradient[1]
     for number, offset in enumerate(OFFSETS):
         pl.when(there[offset])(near[number].wait_send)
-        pl.when(there[offset])(home[number].wait_send)
-    for copy in sums:
-        copy.wait()
-    total = groups[0]
-    for g in range(1, group_count):
-        total += groups[g]
-    out[...] = region[2, pl.ds(PAD, ROWS), :] - STEP * total
+    for offset, copy in home:
+        if offset == 0:
+            copy.wait_recv()
+        else:
+            pl.when(there[-offset])(copy.wait_recv)
+    lane = lax.broadcasted_iota(I32, (ROWS, COLS), 1)
+    total = jnp.zeros((ROWS, COLS), F32)
+    for g in range(group_count):
+        total += arrived[g, 1]
+        total += jnp.where(there[1], arrived[g, 0], 0.0)
+        total += jnp.where(there[-1], arrived[g, 2], 0.0)
+        total += jnp.where(there[2] & (lane >= COLS - ROWS), unpack(far_arrived[g, 0], True), 0.0)
+        total += jnp.where(there[-2] & (lane < ROWS), unpack(far_arrived[g, 1], False), 0.0)
+    out[...] = sky_here[...] - STEP * total
+    for offset, copy in home:
+        if offset == 0:
+            copy.wait_send()
+        else:
+            pl.when(there[offset])(copy.wait_send)
 
 
 def per_device(sky, psf_basis, item_tile, warp_corner, warp_weight, psf_coeff, observed, inv_var):
@@ -303,8 +336,10 @@
             pltpu.VMEM(observed.shape, BF16),
             pltpu.VMEM(inv_var.shape, BF16),
             pltpu.VMEM((5, ROWS + 2 * PAD, COLS), F32),
-            pltpu.VMEM((4, ROWS, COLS), F32),
-            pltpu.VMEM((group_count, ROWS, COLS), F32),
+            pltpu.VMEM((2, 8, COLS), F32),
+            pltpu.VMEM((2, 8, COLS), F32),
+            pltpu.VMEM((group_count, 3, ROWS, COLS), F32),
+            pltpu.VMEM((group_count, 2, 8, COLS), F32),
             pltpu.VMEM((3, ROWS + 2 * PAD, COLS), F32),
             pltpu.VMEM((NPSF, COLS, COLS), F32),
             pltpu.VMEM((NPSF, COLS, COLS), F32),
@@ -318,8 +353,9 @@
             pltpu.VMEM((ITEMS, ROWS, COLS), F32),
             pltpu.VMEM((ITEMS, 4, 2, ROWS, COLS), F32),
             pltpu.VMEM((ITEMS, 2, ROWS + 8, 2 * COLS), F32),
-            pltpu.VMEM((5, ROWS, COLS), F32),
-            dma((6,)), dma((4,)), dma((4,)), dma((4,)), dma((4,)), dma((group_count - 1,)), dma((group_count - 1,)),
+            pltpu.VMEM((3, ROWS, COLS), F32),
+            pltpu.VMEM((2, 8, COLS), F32),
+            dma((6,)), dma((4,)), dma((4,)), dma((group_count, 5)), dma((group_count, 5)),
         ],
         compiler_params=pltpu.CompilerParams(
             collective_id=0, has_side_effects=True, vmem_limit_bytes=62 * 2**20

time: 26.1 us -> 24 us (0.920); the launches traced: 25.9 us -> 23.6 us
  Pallas kernels: 24.6 us -> 22.2 us
    pallas_call x1, Pallas kernels: 24.6 us -> 22.2 us  [per_device(): pl.pallas_call(kernel, out_shape=jax.ShapeDtypeStruct((ROWS, COLS), F32),...]
where the time goes in v3:
time: 24 us; the launch traced here: 23.6 us
  Pallas kernels  22.2 us (92%)
  local copies, waits for them, and re-layouts  1.32 us (6%)
    pallas_call x1, Pallas kernels, per_device(): pl.pallas_call(kernel, out_shape=jax.ShapeDtypeStruct((ROWS, COLS), F32),...  22.2 us
    unnamed x1, local copies, waits for them, and re-layouts  1.32 us

profile of v3, /device:TPU:129, one launch (start us, length us, event | category | flops | bytes accessed | tf_op | source)
XLA Modules:
  0.0 23.6 jit_solution(16282126869252909593)
XLA Ops:
  0.0 22.2 %shard_map.82 = f32[32,128]{1,0:T(8,128)} custom-call(s32[3]{0:T(128)} %tiles.1, f32[32,128]{1,0:T(8,128)} %sky_hbm.1, bf16[1,5,41,41]{3,2,1,0:T(8,128)(2,1)} %psf.1, s32[3,32,128]{2,1,0:T(8,128)} %corner_hbm.1, bf16[3,4,32,128]{3,2,1,0:T(8,128)(2,1)} %weight_hbm.1, bf16[3,5,32,128]{3,2,1,0:T(8,128)(2,1)} %bitcast.1, bf16[3,32,128]{2,1,0:T(8,128)(2,1)} %obs_hbm.1, ...), custom_call_target="tpu_custom_call" | custom-call | tf_op jit(solution)/shard_map/pallas_call | solution.py:327
  22.2 1.3 %copy.10 = f32[32,128]{1,0:T(8,128)} copy(f32[32,128]{1,0:T(8,128)} %shard_map.82) | data formatting | bytes 32768

commit v4 on v3

v4 whole, which is shorter than its diff:
```python
import jax
import jax.numpy as jnp
from jax import lax
from jax.experimental import pallas as pl
from jax.experimental.pallas import tpu as pltpu
from jax.sharding import PartitionSpec as P

F32, BF16, I32 = jnp.float32, jnp.bfloat16, jnp.int32
ROWS, COLS, MARGIN, TAPS, NPSF, ITEMS = 32, 128, 24, 41, 5, 3
EXTENT = COLS + 2 * MARGIN
HALF = TAPS // 2
WIDE = ITEMS * COLS
DEPTH = TAPS * ROWS
GROUPS_OF_4 = (TAPS + 3) // 4
PAD = 8
STEP = 0.25
OFFSETS = (-2, -1, 1, 2)
SLOT = {-2: 0, -1: 1, 0: 2, 1: 3, 2: 4}


def split(value):
    high = value.astype(BF16)
    return high, (value - high.astype(F32)).astype(BF16)


def nt_dot(a, b):
    return lax.dot_general(a, b, (((1,), (1,)), ((), ())), preferred_element_type=F32)


def pack(value, right):
    lane_group = lax.broadcasted_iota(I32, (8, COLS), 1) // ROWS
    packed = jnp.zeros((8, COLS), F32)
    for i in range(4):
        turned = pltpu.roll(value[8 * i : 8 * i + 8], (32 * i + (ROWS if right else 0)) % COLS, 1)
        packed = jnp.where(lane_group == i, turned, packed)
    return packed


def unpack(packed, right):
    return jnp.concatenate(
        [pltpu.roll(packed, (-32 * i - (ROWS if right else 0)) % COLS, 1) for i in range(4)], axis=0
    )


def prepare_hot(corner, hot):
    column = lax.broadcasted_iota(I32, (EXTENT, COLS), 0)

    def hot_rows(step, _):
        n, block = step // 4, lax.rem(step, 4)
        at = corner[n, pl.ds(pl.multiple_of(block * 8, 8), 8), :]
        start = at - ((at * 23832) >> 22) * EXTENT
        for u in range(8):
            row = jnp.broadcast_to(start[u : u + 1], (EXTENT, COLS))
            hot[n, block, :, pl.ds(u * COLS, COLS)] = jnp.where(column == row, 1.0, 0.0).astype(BF16)
        return 0

    lax.fori_loop(0, ITEMS * 4, hot_rows, 0)


def prepare_taps(psf, tap_rows, tap_cols, blur_left, blur_right):
    tap_rows[...] = jnp.zeros_like(tap_rows)
    for k in range(NPSF):
        tap_rows[k, pl.ds(0, TAPS), pl.ds(0, TAPS)] = psf[0, k].astype(F32)
    for k in range(NPSF):
        tap_cols[k] = pltpu.roll(tap_rows[k], 4, 0).T
    lane_group = lax.broadcasted_iota(I32, (8, COLS), 1) // ROWS
    for j in range(GROUPS_OF_4):
        whole = []
        for k in range(NPSF):
            for r0 in range(0, ROWS, 8):
                tile = jnp.zeros((8, COLS), F32)
                for part in range(4):
                    row = jnp.broadcast_to(tap_cols[k, pl.ds(4 * j + part, 1), :], (8, COLS))
                    turned = pltpu.roll(row, (r0 + ROWS * part - HALF - 4) % COLS, 1, stride=1, stride_axis=0)
                    tile = turned if part == 0 else jnp.where(lane_group == part, turned, tile)
                whole.append(tile)
        whole = jnp.concatenate(whole, axis=0)
        blur_left[:, pl.ds(j * COLS, COLS)] = whole.astype(BF16)
        blur_right[pl.ds(j * COLS, COLS), :] = whole.T.astype(BF16)


def join_sides(me, count, region, far_in, sides):
    lane = lax.broadcasted_iota(I32, (ROWS, COLS), 1)
    for t in range(3):
        left = unpack(far_in[1], True) if t == 0 else region[t, pl.ds(PAD, ROWS), :]
        right = unpack(far_in[0], False) if t == 2 else region[t + 2, pl.ds(PAD, ROWS), :]
        if t < 2:
            left = jnp.where(me - 2 + t >= 0, left, 0.0)
        if t > 0:
            right = jnp.where(me + t <= count - 1, right, 0.0)
        sides[t, pl.ds(PAD, ROWS), :] = jnp.where(lane >= COLS // 2, left, right)


def warp(n, me, tiles, corner, weight, region, sides, warped):
    t = jnp.clip(tiles[n] - (me - 1), 0, 2)
    for r0 in range(0, ROWS, 8):
        at = corner[n, pl.ds(r0, 8), :]
        q = (at * 23832) >> 22
        p = at - q * EXTENT
        rel = q - (lax.broadcasted_iota(I32, (8, COLS), 0) + r0) + 3
        total = jnp.zeros((8, COLS), F32)
        for dp in range(2):
            index = (p + (dp + COLS - MARGIN)) & (COLS - 1)
            middle = (p + dp >= MARGIN) & (p + dp < MARGIN + COLS)
            upper = jnp.zeros((8, COLS), F32)
            lower = jnp.zeros((8, COLS), F32)
            for o in range(8):
                rows = pl.ds(r0 + (PAD - 3 + o), 8)
                inside = jnp.take_along_axis(region[t + 1, rows, :], index, axis=1)
                beside = jnp.take_along_axis(sides[t, rows, :], index, axis=1)
                found = jnp.where(middle, inside, beside)
                if o < 7:
                    upper = jnp.where(rel == o, found, upper)
                if o > 0:
                    lower = jnp.where(rel == o - 1, found, lower)
            total += weight[n, dp, pl.ds(r0, 8), :].astype(F32) * upper
            total += weight[n, 2 + dp, pl.ds(r0, 8), :].astype(F32) * lower
        warped[n, pl.ds(r0, 8), :] = total


def blur(n, coeff, obs, ivar, warped, lifted, blur_left, misfit_parts):
    lane = lax.broadcasted_iota(I32, (ROWS, COLS), 1)
    for b in range(TAPS):
        source = lane + (b - HALF)
        inside = (source >= 0) & (source < COLS)
        value = warped[n]
        if b != HALF:
            value = jnp.where(inside, pltpu.roll(value, (HALF - b) % COLS, 1), 0.0)
        high, low = split(value)
        lifted[n, pl.ds(b * ROWS, ROWS), pl.ds(0, COLS)] = high
        lifted[n, pl.ds(b * ROWS, ROWS), pl.ds(COLS, COLS)] = low
    both = jnp.dot(blur_left[:, pl.ds(0, DEPTH)], lifted[n], preferred_element_type=F32)
    blurred = both[:, :COLS] + both[:, COLS:]
    predicted = jnp.zeros((ROWS, COLS), F32)
    for k in range(NPSF):
        predicted += coeff[n, k].astype(F32) * blurred[k * ROWS : (k + 1) * ROWS]
    misfit = ivar[n].astype(F32) * (predicted - obs[n].astype(F32))
    for k in range(NPSF):
        high, low = split(coeff[n, k].astype(F32) * misfit)
        misfit_parts[n, pl.ds(k * ROWS, ROWS), pl.ds(0, COLS)] = high
        misfit_parts[n, pl.ds(k * ROWS, ROWS), pl.ds(COLS, COLS)] = low


def back(n, blur_right, misfit_parts, spread, backward):
    lane = lax.broadcasted_iota(I32, (ROWS, COLS), 1)
    spread[n] = jnp.dot(blur_right[pl.ds(0, DEPTH), :], misfit_parts[n], preferred_element_type=F32)
    total = jnp.zeros((ROWS, COLS), F32)
    for b in range(TAPS):
        source = lane - (b - HALF)
        inside = (source >= 0) & (source < COLS)
        value = spread[n, pl.ds(b * ROWS, ROWS), pl.ds(0, COLS)] + spread[n, pl.ds(b * ROWS, ROWS), pl.ds(COLS, COLS)]
        if b != HALF:
            value = jnp.where(inside, pltpu.roll(value, (b - HALF) % COLS, 1), 0.0)
        total += value
    backward[n] = total


def scatter(n, corner, weight, backward, hot, parts, window_grad):
    target = lax.broadcasted_iota(I32, (16, COLS), 0)
    for j in range(4):
        value = weight[n, j].astype(F32) * backward[n]
        high = value.astype(BF16).astype(F32)
        parts[n, j, 0] = high
        parts[n, j, 1] = value - high
    for block in range(4):
        r0 = block * 8
        q = ((corner[n, pl.ds(r0, 8), :] * 23832) >> 22) - (r0 - 4)
        columns = []
        for u in range(8):
            row = jnp.broadcast_to(q[u : u + 1], (16, COLS))
            first, second = target == row, target == row + 1
            stack = []
            for dp in range(2):
                for half in range(2):
                    one_up = jnp.broadcast_to(parts[n, dp, half, pl.ds(r0 + u, 1), :], (16, COLS))
                    one_low = jnp.broadcast_to(parts[n, 2 + dp, half, pl.ds(r0 + u, 1), :], (16, COLS))
                    stack.append(jnp.where(first, one_up, jnp.where(second, one_low, 0.0)).astype(BF16))
            columns.append(jnp.concatenate(stack, axis=0))
        values = jnp.concatenate(columns, axis=1)
        found = nt_dot(values, hot[n, block])
        for dp in range(2):
            part = found[dp * 32 : dp * 32 + 16] + found[dp * 32 + 16 : dp * 32 + 32]
            window_grad[n, dp, pl.ds(r0, 16), pl.ds(0, EXTENT)] += part


def gather_tiles(me, tiles, window_grad, gradient, far_gradient):
    lane = lax.broadcasted_iota(I32, (ROWS, COLS), 1)
    left_lanes = lane >= COLS // 2
    totals = [jnp.zeros((ROWS, COLS), F32) for _ in range(5)]
    for n in range(ITEMS):
        t = jnp.clip(tiles[n] - (me - 1), 0, 2)
        whole = pltpu.roll(window_grad[n, 0, pl.ds(4, ROWS), :], COLS - MARGIN, 1)
        whole += pltpu.roll(window_grad[n, 1, pl.ds(4, ROWS), :], COLS - MARGIN + 1, 1)
        beside, inside = whole[:, :COLS], whole[:, COLS:]
        left = jnp.where(left_lanes, beside, 0.0)
        right = jnp.where(left_lanes, 0.0, beside)
        for s in range(5):
            if n == 0 and s not in (1, 2, 3):
                continue
            if s - 1 in (0, 1, 2):
                totals[s] += jnp.where(t == s - 1, inside, 0.0)
            if s in (0, 1, 2):
                totals[s] += jnp.where(t == s, left, 0.0)
            if s - 2 in (0, 1, 2):
                totals[s] += jnp.where(t == s - 2, right, 0.0)
    for s in range(3):
        gradient[s] = totals[s + 1]
    far_gradient[0] = pack(totals[0], True)
    far_gradient[1] = pack(totals[4], False)


def kernel(tiles_hbm, sky_hbm, psf_hbm, corner_hbm, weight_hbm, coeff_hbm, obs_hbm, ivar_hbm, out,
           tiles, psf, corner, weight, coeff, obs, ivar,
           region, far_out, far_in, arrived, far_arrived, sides, tap_rows, tap_cols, blur_left, blur_right,
           hot, warped, lifted, misfit_parts, spread, backward, parts, window_grad, gradient, far_gradient,
           load, near_send, near_recv, back_send, back_recv, ready):
    me, grp = lax.axis_index("tile"), lax.axis_index("grp")
    count, group_count = lax.axis_size("tile"), lax.axis_size("grp")
    mesh_id = pl.DeviceIdType.MESH
    there = {offset: (me + offset >= 0) & (me + offset <= count - 1) for offset in OFFSETS}
    others = [lax.rem(grp + step, group_count) for step in range(group_count)]
    barrier = pltpu.get_barrier_semaphore()
    for offset in OFFSETS:
        @pl.when(there[offset])
        def _():
            pl.semaphore_signal(barrier, inc=1, device_id=(grp, me + offset), device_id_type=mesh_id)
    for other in others[1:]:
        pl.semaphore_signal(barrier, inc=1, device_id=(other, me), device_id_type=mesh_id)
    sky_here = region.at[2, pl.ds(PAD, ROWS), :]
    pairs = ((sky_hbm, sky_here), (corner_hbm, corner), (weight_hbm, weight),
             (coeff_hbm, coeff), (obs_hbm, obs), (ivar_hbm, ivar), (tiles_hbm, tiles), (psf_hbm, psf))
    loads = [pltpu.make_async_copy(a, b, load.at[i]) for i, (a, b) in enumerate(pairs)]
    for copy in loads:
        copy.start()
    loads[0].wait()
    far_out[0] = pack(sky_here[...], False)
    far_out[1] = pack(sky_here[...], True)
    loads[1].wait()
    prepare_hot(corner, hot)
    neighbours = jnp.minimum(me, 2) + jnp.minimum(count - 1 - me, 2)
    pl.semaphore_wait(barrier, neighbours + group_count - 1)

    near = []
    for number, offset in enumerate(OFFSETS):
        side = 0 if offset < 0 else 1
        near.append(pltpu.make_async_remote_copy(
            src_ref=sky_here if abs(offset) == 1 else far_out.at[side],
            dst_ref=region.at[SLOT[-offset], pl.ds(PAD, ROWS), :] if abs(offset) == 1 else far_in.at[side],
            send_sem=near_send.at[number],
            recv_sem=near_recv.at[number],
            device_id=(grp, me + offset),
            device_id_type=mesh_id,
        ))
    for number in (0, 3, 1, 2):
        pl.when(there[OFFSETS[number]])(near[number].start)
    for step, other in enumerate(others[1:]):
        pl.semaphore_signal(ready.at[step], inc=1, device_id=(other, me), device_id_type=mesh_id)
    window_grad[...] = jnp.zeros_like(window_grad)
    loads[7].wait()
    prepare_taps(psf, tap_rows, tap_cols, blur_left, blur_right)
    for copy in loads[2:7]:
        copy.wait()
    for number, offset in enumerate(OFFSETS):
        pl.when(there[-offset])(near[number].wait_recv)
    for step in range(group_count - 1):
        pl.semaphore_wait(ready.at[step], 1)
    join_sides(me, count, region, far_in, sides)
    for n in range(ITEMS):
        warp(n, me, tiles, corner, weight, region, sides, warped)
    for n in range(ITEMS):
        blur(n, coeff, obs, ivar, warped, lifted, blur_left, misfit_parts)
    for n in range(ITEMS):
        back(n, blur_right, misfit_parts, spread, backward)
    for n in range(ITEMS):
        scatter(n, corner, weight, backward, hot, parts, window_grad)
    gather_tiles(me, tiles, window_grad, gradient, far_gradient)

    home = {}
    for offset in (-2, 2, -1, 1, 0):
        number = OFFSETS.index(offset) if offset else 4
        if abs(offset) == 2:
            source, target = far_gradient.at[number // 3], far_arrived.at[grp, number // 3]
        else:
            source, target = gradient.at[offset + 1], arrived.at[grp, offset + 1]
        home[offset] = [
            pltpu.make_async_remote_copy(
                src_ref=source,
                dst_ref=target,
                send_sem=back_send.at[step, number],
                recv_sem=back_recv.at[step, number],
                device_id=(others[step], me + offset),
                device_id_type=mesh_id,
            )
            for step in range(0 if offset else 1, group_count)
        ]

        def leave_for(offset=offset):
            for copy in home[offset]:
                copy.start()

        if offset:
            pl.when(there[offset])(leave_for)
        else:
            leave_for()
    arrived[grp, 1] = gradient[1]
    for number, offset in enumerate(OFFSETS):
        pl.when(there[offset])(near[number].wait_send)
    for offset in (0, *OFFSETS):
        def arrive(offset=offset):
            for copy in home[offset]:
                copy.wait_recv()

        if offset:
            pl.when(there[-offset])(arrive)
        else:
            arrive()
    lane = lax.broadcasted_iota(I32, (ROWS, COLS), 1)
    total = jnp.zeros((ROWS, COLS), F32)
    for g in range(group_count):
        total += arrived[g, 1]
        total += jnp.where(there[1], arrived[g, 0], 0.0)
        total += jnp.where(there[-1], arrived[g, 2], 0.0)
        total += jnp.where(there[2] & (lane >= COLS - ROWS), unpack(far_arrived[g, 0], True), 0.0)
        total += jnp.where(there[-2] & (lane < ROWS), unpack(far_arrived[g, 1], False), 0.0)
    out[...] = sky_here[...] - STEP * total
    for offset in (0, *OFFSETS):
        def leave(offset=offset):
            for copy in home[offset]:
                copy.wait_send()

        if offset:
            pl.when(there[offset])(leave)
        else:
            leave()


def per_device(sky, psf_basis, item_tile, warp_corner, warp_weight, psf_coeff, observed, inv_var):
    group_count = lax.axis_size("grp")
    vmem = pl.BlockSpec(memory_space=pltpu.VMEM)
    dma = pltpu.SemaphoreType.DMA
    hbm = pl.BlockSpec(memory_space=pltpu.HBM)
    coeff = psf_coeff.transpose(0, 2, 1, 3)
    return pl.pallas_call(
        kernel,
        out_shape=jax.ShapeDtypeStruct((ROWS, COLS), F32),
        in_specs=[hbm] * 8,
        out_specs=vmem,
        scratch_shapes=[
            pltpu.SMEM(item_tile.shape, I32),
            pltpu.VMEM(psf_basis.shape, BF16),
            pltpu.VMEM(warp_corner.shape, I32),
            pltpu.VMEM(warp_weight.shape, BF16),
            pltpu.VMEM(coeff.shape, BF16),
            pltpu.VMEM(observed.shape, BF16),
            pltpu.VMEM(inv_var.shape, BF16),
            pltpu.VMEM((5, ROWS + 2 * PAD, COLS), F32),
            pltpu.VMEM((2, 8, COLS), F32),
            pltpu.VMEM((2, 8, COLS), F32),
            pltpu.VMEM((group_count, 3, ROWS, COLS), F32),
            pltpu.VMEM((group_count, 2, 8, COLS), F32),
            pltpu.VMEM((3, ROWS + 2 * PAD, COLS), F32),
            pltpu.VMEM((NPSF, COLS, COLS), F32),
            pltpu.VMEM((NPSF, COLS, COLS), F32),
            pltpu.VMEM((NPSF * ROWS, GROUPS_OF_4 * COLS), BF16),
            pltpu.VMEM((GROUPS_OF_4 * COLS, NPSF * ROWS), BF16),
            pltpu.VMEM((ITEMS, 4, EXTENT, 8 * COLS), BF16),
            pltpu.VMEM((ITEMS, ROWS, COLS), F32),
            pltpu.VMEM((ITEMS, DEPTH, 2 * COLS), BF16),
            pltpu.VMEM((ITEMS, NPSF * ROWS, 2 * COLS), BF16),
            pltpu.VMEM((ITEMS, DEPTH, 2 * COLS), F32),
            pltpu.VMEM((ITEMS, ROWS, COLS), F32),
            pltpu.VMEM((ITEMS, 4, 2, ROWS, COLS), F32),
            pltpu.VMEM((ITEMS, 2, ROWS + 8, 2 * COLS), F32),
            pltpu.VMEM((3, ROWS, COLS), F32),
            pltpu.VMEM((2, 8, COLS), F32),
            dma((8,)), dma((4,)), dma((4,)), dma((group_count, 5)), dma((group_count, 5)),
            pltpu.SemaphoreType.REGULAR((group_count - 1,)),
        ],
        compiler_params=pltpu.CompilerParams(
            collective_id=0, has_side_effects=True, vmem_limit_bytes=int(53.91 * 2**20)
        ),
    )(item_tile, sky, psf_basis, warp_corner, warp_weight, coeff, observed, inv_var)


def solution(mesh):
    return jax.shard_map(
        per_device,
        mesh=mesh,
        in_specs=(
            P(None, "tile"),
            P("grp", None, None, None),
            P(("grp", "tile")),
            P(("grp", "tile"), None, None),
            P(("grp", "tile"), None, None, None),
            P(("grp", "tile"), None, None, None),
            P(("grp", "tile"), None, None),
            P(("grp", "tile"), None, None),
        ),
        out_specs=P(None, "tile"),
        check_vma=False,
    )
```

time: 24 us -> 21.6 us (0.900); the launches traced: 23.6 us -> 21.5 us
  Pallas kernels: 22.2 us -> 20.2 us
    pallas_call x1, Pallas kernels: 22.2 us -> 20.2 us  [per_device(): pl.pallas_call(kernel, out_shape=jax.ShapeDtypeStruct((ROWS, COLS), F32),...]
    unnamed x1 -> x3, local copies, waits for them, and re-layouts: 1.32 us -> 1.26 us
where the time goes in v4:
time: 21.6 us; the launch traced here: 21.5 us
  Pallas kernels  20.2 us (94%)
  local copies, waits for them, and re-layouts  1.26 us (6%)
    pallas_call x1, Pallas kernels, per_device(): pl.pallas_call(kernel, out_shape=jax.ShapeDtypeStruct((ROWS, COLS), F32),...  20.2 us
    unnamed x3, local copies, waits for them, and re-layouts  1.26 us

profile of v4, /device:TPU:129, one launch (start us, length us, event | category | flops | bytes accessed | tf_op | source)
XLA Modules:
  0.0 21.5 jit_solution(4561950858251664882)
XLA Ops:
  0.0 0.0 copy-start
  0.0 0.7 %copy-done = s32[3]{0:T(128)S(1)} copy-done((s32[3]{0:T(128)S(1)}, s32[3]{0:T(128)}, u32[]{:S(2)}) %copy-start) | copy-done | bytes 36
  0.7 20.2 %shard_map.82 = f32[32,128]{1,0:T(8,128)S(1)} custom-call(s32[3]{0:T(128)S(1)} %copy-done, f32[32,128]{1,0:T(8,128)} %sky_hbm.1, bf16[1,5,41,41]{3,2,1,0:T(8,128)(2,1)} %psf_hbm.1, s32[3,32,128]{2,1,0:T(8,128)} %corner_hbm.1, bf16[3,4,32,128]{3,2,1,0:T(8,128)(2,1)} %weight_hbm.1, bf16[3,5,32,128]{3,2,1,0:T(8,128)(2,1)} %bitcast.1, ...), custom_call_target="tpu_custom_call" | custom-call | tf_op jit(solution)/shard_map/pallas_call | solution.py:343
  20.8 0.6 %copy.10 = f32[32,128]{1,0:T(8,128)} copy(f32[32,128]{1,0:T(8,128)S(1)} %shard_map.82) | data formatting | bytes 32768
Async XLA Ops:
  0.0 0.7 %copy-start = (s32[3]{0:T(128)S(1)}, s32[3]{0:T(128)}, u32[]{:S(2)}) copy-start(s32[3]{0:T(128)} %tiles_hbm.1) | copy-start | bytes 40

commit v5 on v4

--- a/solution.py
+++ b/solution.py
@@ -1,3 +1,5 @@
+import functools
+
 import jax
 import jax.numpy as jnp
 from jax import lax
@@ -235,8 +237,6 @@
     loads[0].wait()
     far_out[0] = pack(sky_here[...], False)
     far_out[1] = pack(sky_here[...], True)
-    loads[1].wait()
-    prepare_hot(corner, hot)
     neighbours = jnp.minimum(me, 2) + jnp.minimum(count - 1 - me, 2)
     pl.semaphore_wait(barrier, neighbours + group_count - 1)
 
@@ -256,6 +256,8 @@
     for step, other in enumerate(others[1:]):
         pl.semaphore_signal(ready.at[step], inc=1, device_id=(other, me), device_id_type=mesh_id)
     window_grad[...] = jnp.zeros_like(window_grad)
+    loads[1].wait()
+    prepare_hot(corner, hot)
     loads[7].wait()
     prepare_taps(psf, tap_rows, tap_cols, blur_left, blur_right)
     for copy in loads[2:7]:
@@ -286,8 +288,8 @@
             pltpu.make_async_remote_copy(
                 src_ref=source,
                 dst_ref=target,
-                send_sem=back_send.at[step, number],
-                recv_sem=back_recv.at[step, number],
+                send_sem=back_send.at[number],
+                recv_sem=back_recv.at[number],
                 device_id=(others[step], me + offset),
                 device_id_type=mesh_id,
             )
@@ -305,15 +307,18 @@
     arrived[grp, 1] = gradient[1]
     for number, offset in enumerate(OFFSETS):
         pl.when(there[offset])(near[number].wait_send)
-    for offset in (0, *OFFSETS):
-        def arrive(offset=offset):
-            for copy in home[offset]:
-                copy.wait_recv()
-
-        if offset:
-            pl.when(there[-offset])(arrive)
+    def wait_all(semaphores, offset):
+        number = OFFSETS.index(offset) if offset else 4
+        first = 0 if offset else 1
+        if abs(offset) == 2:
+            whole = far_arrived.at[pl.ds(first, group_count - first), number // 3]
         else:
-            arrive()
+            whole = arrived.at[pl.ds(first, group_count - first), offset + 1]
+        pltpu.make_async_copy(whole, whole, semaphores.at[number]).wait()
+
+    wait_all(back_recv, 0)
+    for offset in OFFSETS:
+        pl.when(there[-offset])(functools.partial(wait_all, back_recv, offset))
     lane = lax.broadcasted_iota(I32, (ROWS, COLS), 1)
     total = jnp.zeros((ROWS, COLS), F32)
     for g in range(group_count):
@@ -323,15 +328,9 @@
         total += jnp.where(there[2] & (lane >= COLS - ROWS), unpack(far_arrived[g, 0], True), 0.0)
         total += jnp.where(there[-2] & (lane < ROWS), unpack(far_arrived[g, 1], False), 0.0)
     out[...] = sky_here[...] - STEP * total
-    for offset in (0, *OFFSETS):
-        def leave(offset=offset):
-            for copy in home[offset]:
-                copy.wait_send()
-
-        if offset:
-            pl.when(there[offset])(leave)
-        else:
-            leave()
+    wait_all(back_send, 0)
+    for offset in OFFSETS:
+        pl.when(there[offset])(functools.partial(wait_all, back_send, offset))
 
 
 def per_device(sky, psf_basis, item_tile, warp_corner, warp_weight, psf_coeff, observed, inv_var):
@@ -373,7 +372,7 @@
             pltpu.VMEM((ITEMS, 2, ROWS + 8, 2 * COLS), F32),
             pltpu.VMEM((3, ROWS, COLS), F32),
             pltpu.VMEM((2, 8, COLS), F32),
-            dma((8,)), dma((4,)), dma((4,)), dma((group_count, 5)), dma((group_count, 5)),
+            dma((8,)), dma((4,)), dma((4,)), dma((5,)), dma((5,)),
             pltpu.SemaphoreType.REGULAR((group_count - 1,)),
         ],
         compiler_params=pltpu.CompilerParams(

time: 21.6 us -> 21.3 us (0.986)
  Pallas kernels: 20.2 us -> 19.9 us
    pallas_call x1, Pallas kernels: 20.2 us -> 19.9 us  [per_device(): pl.pallas_call(kernel, out_shape=jax.ShapeDtypeStruct((ROWS, COLS), F32),...]
where the time goes in v5:
time: 21.3 us; the launch traced here: 21.2 us
  Pallas kernels  19.9 us (93%)
  local copies, waits for them, and re-layouts  1.26 us (6%)
    pallas_call x1, Pallas kernels, per_device(): pl.pallas_call(kernel, out_shape=jax.ShapeDtypeStruct((ROWS, COLS), F32),...  19.9 us
    unnamed x3, local copies, waits for them, and re-layouts  1.26 us

profile of v5, /device:TPU:129, one launch (start us, length us, event | category | flops | bytes accessed | tf_op | source)
XLA Modules:
  0.0 21.2 jit_solution(6186658768334089732)
XLA Ops:
  0.0 0.0 copy-start
  0.0 0.7 %copy-done = s32[3]{0:T(128)S(1)} copy-done((s32[3]{0:T(128)S(1)}, s32[3]{0:T(128)}, u32[]{:S(2)}) %copy-start) | copy-done | bytes 36
  0.7 19.9 %shard_map.82 = f32[32,128]{1,0:T(8,128)S(1)} custom-call(s32[3]{0:T(128)S(1)} %copy-done, f32[32,128]{1,0:T(8,128)} %sky_hbm.1, bf16[1,5,41,41]{3,2,1,0:T(8,128)(2,1)} %psf_hbm.1, s32[3,32,128]{2,1,0:T(8,128)} %corner_hbm.1, bf16[3,4,32,128]{3,2,1,0:T(8,128)(2,1)} %weight_hbm.1, bf16[3,5,32,128]{3,2,1,0:T(8,128)(2,1)} %bitcast.1, ...), custom_call_target="tpu_custom_call" | custom-call | tf_op jit(solution)/shard_map/pallas_call | solution.py:342
  20.5 0.6 %copy.10 = f32[32,128]{1,0:T(8,128)} copy(f32[32,128]{1,0:T(8,128)S(1)} %shard_map.82) | data formatting | bytes 32768
Async XLA Ops:
  0.0 0.7 %copy-start = (s32[3]{0:T(128)S(1)}, s32[3]{0:T(128)}, u32[]{:S(2)}) copy-start(s32[3]{0:T(128)} %tiles_hbm.1) | copy-start | bytes 40

commit v6 on v5

--- a/solution.py
+++ b/solution.py
@@ -185,30 +185,26 @@
             window_grad[n, dp, pl.ds(r0, 16), pl.ds(0, EXTENT)] += part
 
 
-def gather_tiles(me, tiles, window_grad, gradient, far_gradient):
-    lane = lax.broadcasted_iota(I32, (ROWS, COLS), 1)
-    left_lanes = lane >= COLS // 2
-    totals = [jnp.zeros((ROWS, COLS), F32) for _ in range(5)]
+def window_parts(me, tiles, window_grad):
+    left_lanes = lax.broadcasted_iota(I32, (ROWS, COLS), 1) >= COLS // 2
+    found = []
     for n in range(ITEMS):
-        t = jnp.clip(tiles[n] - (me - 1), 0, 2)
         whole = pltpu.roll(window_grad[n, 0, pl.ds(4, ROWS), :], COLS - MARGIN, 1)
         whole += pltpu.roll(window_grad[n, 1, pl.ds(4, ROWS), :], COLS - MARGIN + 1, 1)
         beside, inside = whole[:, :COLS], whole[:, COLS:]
         left = jnp.where(left_lanes, beside, 0.0)
         right = jnp.where(left_lanes, 0.0, beside)
-        for s in range(5):
-            if n == 0 and s not in (1, 2, 3):
-                continue
-            if s - 1 in (0, 1, 2):
-                totals[s] += jnp.where(t == s - 1, inside, 0.0)
-            if s in (0, 1, 2):
-                totals[s] += jnp.where(t == s, left, 0.0)
-            if s - 2 in (0, 1, 2):
-                totals[s] += jnp.where(t == s - 2, right, 0.0)
-    for s in range(3):
-        gradient[s] = totals[s + 1]
-    far_gradient[0] = pack(totals[0], True)
-    far_gradient[1] = pack(totals[4], False)
+        found.append((jnp.clip(tiles[n] - (me - 1), 0, 2), left, inside, right))
+    return found
+
+
+def tile_total(found, slot):
+    total = jnp.zeros((ROWS, COLS), F32)
+    for n, (t, *three) in enumerate(found):
+        for place, part in enumerate(three):
+            if 0 <= slot - place <= 2 and (n > 0 or slot - place == 1):
+                total += jnp.where(t == slot - place, part, 0.0)
+    return total
 
 
 def kernel(tiles_hbm, sky_hbm, psf_hbm, corner_hbm, weight_hbm, coeff_hbm, obs_hbm, ivar_hbm, out,
@@ -275,10 +271,15 @@
         back(n, blur_right, misfit_parts, spread, backward)
     for n in range(ITEMS):
         scatter(n, corner, weight, backward, hot, parts, window_grad)
-    gather_tiles(me, tiles, window_grad, gradient, far_gradient)
+    found = window_parts(me, tiles, window_grad)
+    far_gradient[0] = pack(tile_total(found, 0), True)
+    far_gradient[1] = pack(tile_total(found, 4), False)
 
     home = {}
     for offset in (-2, 2, -1, 1, 0):
+        if offset == -1:
+            for slot in range(3):
+                gradient[slot] = tile_total(found, slot + 1)
         number = OFFSETS.index(offset) if offset else 4
         if abs(offset) == 2:
             source, target = far_gradient.at[number // 3], far_arrived.at[grp, number // 3]

time: 21.3 us -> 21.4 us (level)
  no operation moved by 1% of the time
where the time goes in v6:
time: 21.4 us; the launch traced here: 21.2 us
  Pallas kernels  19.9 us (93%)
  local copies, waits for them, and re-layouts  1.26 us (6%)
    pallas_call x1, Pallas kernels, per_device(): pl.pallas_call(kernel, out_shape=jax.ShapeDtypeStruct((ROWS, COLS), F32),...  19.9 us
    unnamed x3, local copies, waits for them, and re-layouts  1.26 us

profile of v6, /device:TPU:129, one launch (start us, length us, event | category | flops | bytes accessed | tf_op | source)
XLA Modules:
  0.0 21.2 jit_solution(3251313183510428560)
XLA Ops:
  0.0 0.0 copy-start
  0.0 0.7 %copy-done = s32[3]{0:T(128)S(1)} copy-done((s32[3]{0:T(128)S(1)}, s32[3]{0:T(128)}, u32[]{:S(2)}) %copy-start) | copy-done | bytes 36
  0.7 19.9 %shard_map.82 = f32[32,128]{1,0:T(8,128)S(1)} custom-call(s32[3]{0:T(128)S(1)} %copy-done, f32[32,128]{1,0:T(8,128)} %sky_hbm.1, bf16[1,5,41,41]{3,2,1,0:T(8,128)(2,1)} %psf_hbm.1, s32[3,32,128]{2,1,0:T(8,128)} %corner_hbm.1, bf16[3,4,32,128]{3,2,1,0:T(8,128)(2,1)} %weight_hbm.1, bf16[3,5,32,128]{3,2,1,0:T(8,128)(2,1)} %bitcast.1, ...), custom_call_target="tpu_custom_call" | custom-call | tf_op jit(solution)/shard_map/pallas_call | solution.py:343
  20.6 0.6 %copy.10 = f32[32,128]{1,0:T(8,128)} copy(f32[32,128]{1,0:T(8,128)S(1)} %shard_map.82) | data formatting | bytes 32768
Async XLA Ops:
  0.0 0.7 %copy-start = (s32[3]{0:T(128)S(1)}, s32[3]{0:T(128)}, u32[]{:S(2)}) copy-start(s32[3]{0:T(128)} %tiles_hbm.1) | copy-start | bytes 40

commit v7 on v6

--- a/solution.py
+++ b/solution.py
@@ -377,7 +377,7 @@
             pltpu.SemaphoreType.REGULAR((group_count - 1,)),
         ],
         compiler_params=pltpu.CompilerParams(
-            collective_id=0, has_side_effects=True, vmem_limit_bytes=int(53.91 * 2**20)
+            collective_id=0, has_side_effects=True, vmem_limit_bytes=62 * 2**20
         ),
     )(item_tile, sky, psf_basis, warp_corner, warp_weight, coeff, observed, inv_var)
 

time: 21.4 us -> 22.1 us (1.033)
  Pallas kernels: 19.9 us -> 20.5 us
    pallas_call x1, Pallas kernels: 19.9 us -> 20.5 us  [per_device(): pl.pallas_call(kernel, out_shape=jax.ShapeDtypeStruct((ROWS, COLS), F32),...]
    unnamed x3 -> x1, local copies, waits for them, and re-layouts: 1.26 us -> 1.32 us
where the time goes in v7:
time: 22.1 us; the launch traced here: 21.8 us
  Pallas kernels  20.5 us (93%)
  local copies, waits for them, and re-layouts  1.32 us (6%)
    pallas_call x1, Pallas kernels, per_device(): pl.pallas_call(kernel, out_shape=jax.ShapeDtypeStruct((ROWS, COLS), F32),...  20.5 us
    unnamed x1, local copies, waits for them, and re-layouts  1.32 us

profile of v7, /device:TPU:129, one launch (start us, length us, event | category | flops | bytes accessed | tf_op | source)
XLA Modules:
  0.0 21.8 jit_solution(620112893169183457)
XLA Ops:
  0.0 20.5 %shard_map.82 = f32[32,128]{1,0:T(8,128)} custom-call(s32[3]{0:T(128)} %tiles_hbm.1, f32[32,128]{1,0:T(8,128)} %sky_hbm.1, bf16[1,5,41,41]{3,2,1,0:T(8,128)(2,1)} %psf_hbm.1, s32[3,32,128]{2,1,0:T(8,128)} %corner_hbm.1, bf16[3,4,32,128]{3,2,1,0:T(8,128)(2,1)} %weight_hbm.1, bf16[3,5,32,128]{3,2,1,0:T(8,128)(2,1)} %bitcast.1, bf16[3,32,128]{2,1,0:T(8,128)(2,1)} %obs_hbm.1, ...), custom_call_target="tpu_custom_call" | custom-call | tf_op jit(solution)/shard_map/pallas_call | solution.py:343
  20.5 1.3 %copy.10 = f32[32,128]{1,0:T(8,128)} copy(f32[32,128]{1,0:T(8,128)} %shard_map.82) | data formatting | bytes 32768

commit v8 on v6

--- a/solution.py
+++ b/solution.py
@@ -294,7 +294,7 @@
                 device_id=(others[step], me + offset),
                 device_id_type=mesh_id,
             )
-            for step in range(0 if offset else 1, group_count)
+            for step in (*range(1, group_count), *((0,) if offset else ()))
         ]
 
         def leave_for(offset=offset):

time: 21.4 us -> 21.2 us (level)
  no operation moved by 1% of the time
where the time goes in v8:
time: 21.2 us; the launch traced here: 21 us
  Pallas kernels  19.7 us (93%)
  local copies, waits for them, and re-layouts  1.26 us (6%)
    pallas_call x1, Pallas kernels, per_device(): pl.pallas_call(kernel, out_shape=jax.ShapeDtypeStruct((ROWS, COLS), F32),...  19.7 us
    unnamed x3, local copies, waits for them, and re-layouts  1.26 us

profile of v8, /device:TPU:129, one launch (start us, length us, event | category | flops | bytes accessed | tf_op | source)
XLA Modules:
  0.0 21.0 jit_solution(8996797760102460203)
XLA Ops:
  0.0 0.0 copy-start
  0.0 0.7 %copy-done = s32[3]{0:T(128)S(1)} copy-done((s32[3]{0:T(128)S(1)}, s32[3]{0:T(128)}, u32[]{:S(2)}) %copy-start) | copy-done | bytes 36
  0.7 19.7 %shard_map.82 = f32[32,128]{1,0:T(8,128)S(1)} custom-call(s32[3]{0:T(128)S(1)} %copy-done, f32[32,128]{1,0:T(8,128)} %sky_hbm.1, bf16[1,5,41,41]{3,2,1,0:T(8,128)(2,1)} %psf_hbm.1, s32[3,32,128]{2,1,0:T(8,128)} %corner_hbm.1, bf16[3,4,32,128]{3,2,1,0:T(8,128)(2,1)} %weight_hbm.1, bf16[3,5,32,128]{3,2,1,0:T(8,128)(2,1)} %bitcast.1, ...), custom_call_target="tpu_custom_call" | custom-call | tf_op jit(solution)/shard_map/pallas_call | solution.py:343
  20.4 0.6 %copy.10 = f32[32,128]{1,0:T(8,128)} copy(f32[32,128]{1,0:T(8,128)S(1)} %shard_map.82) | data formatting | bytes 32768
Async XLA Ops:
  0.0 0.7 %copy-start = (s32[3]{0:T(128)S(1)}, s32[3]{0:T(128)}, u32[]{:S(2)}) copy-start(s32[3]{0:T(128)} %tiles_hbm.1) | copy-start | bytes 40
